TPU v7x, 256 devices: a whole 4x4x8 slice. The times are simulated.
256 devices in a mesh: ctx: 32 (over y, x, core), head: 8 (over z).
Axes of the slice: x: 4, y: 4, z: 8, core: 2. Of those that a mesh axis runs over, the one named last changes fastest.
Arguments:
- queries: bfloat16 [16384, 2048], P('ctx', 'head'), may hold values from -50 to 50
- key_in: bfloat16 [16384, 2048], P('ctx', 'head'), may hold values from -6 to 6
- values: bfloat16 [16384, 2048], P('ctx', 'head'), may hold values from -6 to 6
- segment: int32 [16384], replicated, may hold values from 0 to 23, never falling along the last dimension, each value on 1 to 4096 neighbouring positions
- tool_ids: int32 [16384], replicated, may hold values from 0 to 256, as said below
- out_weight: bfloat16 [2048, 4096], P('head'), may hold values from -0.125 to 0.125
- grad_mixed: bfloat16 [16384, 4096], P('ctx', 'head'), may hold values from -1.5 to 1.5
Outputs:
- layer_out: bfloat16 [16384, 4096], P('ctx', 'head')
- grad_query: bfloat16 [16384, 2048], P('ctx', 'head')
- grad_key: bfloat16 [16384, 2048], P('ctx', 'head')
- grad_value: bfloat16 [16384, 2048], P('ctx', 'head')
- grad_out_weight: float32 [2048, 4096], P('head', 'ctx')
Inputs may be any that keep to these rules, and one draw needn't show every extreme that they name: `segment`: document ids never fall along the sequence; every document has 1 to 4096 tokens and one has exactly 4096. `tool_ids`: tool block t > 0 is exactly the tokens 64 * (t - 1) to 64 * t - 1; tokens of no tool block carry 0.
All inputs are finite; a program needn't handle non-finite values.
Results may differ from a plain program's by a relative error of at most 0.04.
Values may be sent and summed in bfloat16 or wider, within the bound.
A program may use at most 192 MiB of HBM per device.

v0:
```python
import math

import jax
import jax.numpy as jnp
from jax import lax
from jax.sharding import PartitionSpec as P

HD = 128


NEG = -1e30


def shifted_2(value, axis, by):
    size = lax.axis_size(axis)
    pairs = [(i, i + by) for i in range(size) if 0 <= i + by < size]
    return lax.ppermute(value, axis, pairs)


def visible(seg_query, tool_query, seg_key, tool_key, offset):
    shape_pair = (seg_query.shape[0], seg_key.shape[0])
    row_pos = lax.broadcasted_iota(jnp.int32, shape_pair, 0) + offset
    col_pos = lax.broadcasted_iota(jnp.int32, shape_pair, 1)
    same_doc = seg_query[:, None] == seg_key[None, :]
    tool_ok = (tool_key[None, :] == 0) | (tool_key[None, :] == tool_query[:, None])
    return same_doc & tool_ok & (col_pos <= row_pos)


def body(queries, key_in, values, segment, tool_ids, out_weight, grad_mixed):
    row_count, local_width = queries.shape
    head_count = local_width // HD
    score_scale = 1.0 / math.sqrt(HD)
    span_blocks = lax.axis_size("ctx") // 4
    ctx_rank = lax.axis_index("ctx")
    front_rows = span_blocks * row_count
    seg_pad = jnp.concatenate([jnp.full((front_rows,), -1, jnp.int32), segment])
    tool_pad = jnp.concatenate([jnp.zeros((front_rows,), jnp.int32), tool_ids])
    seg_window = lax.dynamic_slice_in_dim(
        seg_pad, ctx_rank * row_count, front_rows + row_count, 0
    ).reshape(span_blocks + 1, row_count)
    tool_window = lax.dynamic_slice_in_dim(
        tool_pad, ctx_rank * row_count, front_rows + row_count, 0
    ).reshape(span_blocks + 1, row_count)
    seg_query = seg_window[span_blocks]
    tool_query = tool_window[span_blocks]
    remote = []
    for distance in range(span_blocks, 0, -1):
        remote.append(shifted_2((key_in, values), "ctx", distance))
    key_window = jnp.stack([shifted[0] for shifted in remote] + [key_in]).reshape(
        span_blocks + 1, row_count, head_count, HD
    )
    value_window = jnp.stack([shifted[1] for shifted in remote] + [values]).reshape(
        span_blocks + 1, row_count, head_count, HD
    )
    query_heads = queries.reshape(row_count, head_count, HD)

    def block_mask(block_index):
        offset = (span_blocks - block_index) * row_count
        return visible(
            seg_query, tool_query, seg_window[block_index], tool_window[block_index], offset
        )

    def block_scores(block_index, visible_now):
        scores = (
            jnp.einsum(
                "thd,khd->htk",
                query_heads,
                key_window[block_index],
                preferred_element_type=jnp.float32,
            )
            * score_scale
        )
        return jnp.where(visible_now[None], scores, NEG)

    def stats_step(block_index, state_in):
        visible_now = block_mask(block_index)
        run_max, run_sum, score_store = state_in
        scores = block_scores(block_index, visible_now)
        new_max = jnp.maximum(run_max, jnp.max(scores, axis=2))
        new_sum = run_sum * jnp.exp(run_max - new_max) + jnp.sum(
            jnp.exp(scores - new_max[:, :, None]), axis=2
        )
        return (new_max, new_sum, score_store.at[block_index].set(scores))

    start_stats = (
        jnp.full((head_count, row_count), NEG, jnp.float32),
        jnp.zeros((head_count, row_count), jnp.float32),
        jnp.zeros((span_blocks + 1, head_count, row_count, row_count), jnp.float32),
    )
    run_max, run_sum, score_store = lax.fori_loop(0, span_blocks + 1, stats_step, start_stats)
    log_total = run_max + jnp.log(run_sum)

    def block_probs(block_index, visible_now):
        scores = score_store[block_index]
        return jnp.where(visible_now[None], jnp.exp(scores - log_total[:, :, None]), 0.0)

    def attend_step(block_index, state_in):
        visible_now = block_mask(block_index)
        probs_low = block_probs(block_index, visible_now).astype(jnp.bfloat16)
        return state_in + jnp.einsum(
            "htk,khd->thd", probs_low, value_window[block_index], preferred_element_type=jnp.float32
        )

    attended_sum = lax.fori_loop(
        0, span_blocks + 1, attend_step, jnp.zeros((row_count, head_count, HD), jnp.float32)
    )
    attended = attended_sum.reshape(row_count, local_width).astype(jnp.bfloat16)
    partial_out = jnp.dot(attended, out_weight, preferred_element_type=jnp.float32)
    layer_out = lax.psum_scatter(partial_out, "head", scatter_dimension=1, tiled=True).astype(
        jnp.bfloat16
    )
    shard_piece = lax.all_gather(grad_mixed, "head", axis=1, tiled=True)
    grad_sum = lax.dot_general(
        shard_piece, out_weight, (((1,), (1,)), ((), ())), preferred_element_type=jnp.float32
    )
    update = lax.dot_general(
        attended, shard_piece, (((0,), (0,)), ((), ())), preferred_element_type=jnp.float32
    )
    grad_sum, weight_local = (grad_sum, update)
    grad_attended = grad_sum.astype(jnp.bfloat16)
    grad_out_weight = lax.psum_scatter(weight_local, "ctx", scatter_dimension=1, tiled=True)
    grad_heads = grad_attended.reshape(row_count, head_count, HD)
    row_delta = jnp.sum(
        (grad_attended.astype(jnp.float32) * attended.astype(jnp.float32)).reshape(
            row_count, head_count, HD
        ),
        axis=2,
    ).T

    def grad_step(block_index, state_in):
        visible_now = block_mask(block_index)
        query_grad, key_grads, value_grads = state_in
        keys_block = key_window[block_index]
        values_block = value_window[block_index]
        probs = block_probs(block_index, visible_now)
        probs_low = probs.astype(jnp.bfloat16)
        value_grad = jnp.einsum(
            "htk,thd->khd", probs_low, grad_heads, preferred_element_type=jnp.float32
        )
        grad_probs = jnp.einsum(
            "thd,khd->htk", grad_heads, values_block, preferred_element_type=jnp.float32
        )
        grad_scores = (probs * (grad_probs - row_delta[:, :, None]) * score_scale).astype(
            jnp.bfloat16
        )
        query_grad = query_grad + jnp.einsum(
            "htk,khd->thd", grad_scores, keys_block, preferred_element_type=jnp.float32
        )
        key_grad = jnp.einsum(
            "htk,thd->khd", grad_scores, query_heads, preferred_element_type=jnp.float32
        )
        return (
            query_grad,
            key_grads.at[block_index].set(key_grad),
            value_grads.at[block_index].set(value_grad),
        )

    stack_zeros = jnp.zeros((span_blocks + 1, row_count, head_count, HD), jnp.float32)
    start_grads = (jnp.zeros((row_count, head_count, HD), jnp.float32), stack_zeros, stack_zeros)
    query_grad, key_grads, value_grads = lax.fori_loop(0, span_blocks + 1, grad_step, start_grads)
    own_key = key_grads[span_blocks]
    own_value = value_grads[span_blocks]
    for distance in range(1, span_blocks + 1):
        arrived = shifted_2(
            (key_grads[span_blocks - distance], value_grads[span_blocks - distance]),
            "ctx",
            -distance,
        )
        own_key = own_key + arrived[0]
        own_value = own_value + arrived[1]
    grad_query = query_grad.reshape(row_count, local_width).astype(jnp.bfloat16)
    grad_key = own_key.reshape(row_count, local_width).astype(jnp.bfloat16)
    grad_value = own_value.reshape(row_count, local_width).astype(jnp.bfloat16)
    return (layer_out, grad_query, grad_key, grad_value, grad_out_weight)


def solution(mesh):
    in_specs = (
        P("ctx", "head"),
        P("ctx", "head"),
        P("ctx", "head"),
        P(),
        P(),
        P("head", None),
        P("ctx", "head"),
    )
    out_specs = (
        P("ctx", "head"),
        P("ctx", "head"),
        P("ctx", "head"),
        P("ctx", "head"),
        P("head", "ctx"),
    )
    return jax.shard_map(body, mesh=mesh, in_specs=in_specs, out_specs=out_specs, check_vma=False)
```

profile of v0, /device:TPU:244, one launch (start us, length us, event | category | flops | bytes accessed | tf_op | source)
XLA Modules:
  0.0 618.2 jit_solution(2665557463221277107)
XLA Ops:
  24.8 6.1 collective-permute-done
  30.9 5.9 collective-permute-start.4
  42.3 12.1 %collective-permute-start.6 = (bf16[512,256]{0,1:T(8,128)(2,1)S(1)}, bf16[512,256]{0,1:T(8,128)(2,1)S(1)}, u32[]{:S(2)}, u32[]{:S(2)}) collective-permute-start(bf16[512,256]{0,1:T(8,128)(2,1)S(1)} %copy.30), channel_id=1, source_target_pairs={{0,16},{8,24},{16,32},{24,40},{32,48},{40,56},{48,64},{56,72},{64,... | collective-permute-start | bytes 786440 | tf_op jit(solution)/shard_map/ppermute | solution.py:17
  103.1 8.9 %broadcast_in_dim.114 = f32[9,2,512,512]{2,3,1,0:T(8,128)} broadcast(f32[]{:T(128)} %constant.283.clone.1), dimensions={} | broadcast | bytes 18874372 | tf_op jit(solution)/shard_map/broadcast_in_dim | solution.py:88
  111.9 81.0 %while.53 = (s32[]{:T(128)}, f32[2,512]{1,0:T(2,128)S(1)}, f32[2,512]{1,0:T(2,128)S(1)}, f32[9,2,512,512]{2,3,1,0:T(8,128)}, s32[1,512]{1,0:T(1,128)S(1)}, /*ind...) while((s32[]{:T(128)}, f32[2,512]{1,0:T(2,128)S(1)}, ...), condition=%wide.region_4.5_spmd.clone, body=%wide.region_0.4_spmd.clone.sunk | while | flops 138942496 | bytes 19999480 | solution.py:90
  114.9 4.1 fusion.106
  123.9 4.0 fusion.106
  132.9 4.1 fusion.106
  141.9 4.1 fusion.106
  151.0 4.1 fusion.106
  160.0 4.1 fusion.106
  187.0 4.1 fusion.106
  193.0 81.6 %while.54 = (s32[]{:T(128)}, f32[512,2,128]{0,2,1:T(8,128)S(1)}, bf16[9,512,2,128]{1,3,2,0:T(8,128)(2,1)}, s32[1,512]{1,0:T(1,128)S(1)}, s32[9,512]{1,0:T(8,128)...) while((s32[]{:T(128)}, f32[512,2,128]{0,2,1:T(8,128)S(1)}, ...), condition=%wide.region_6.7_spmd.clone, body=%wide.region_5.6_spmd.clone.sunk | while | flops 137626624 | bytes 12347055 | solution.py:104
  278.1 4.7 fusion.62
  283.2 5.4 fusion.63
  294.1 105.5 %while.55 = (s32[]{:T(128)}, f32[512,2,128]{0,2,1:T(8,128)S(1)}, f32[9,512,2,128]{3,1,2,0:T(8,128)}, f32[9,512,2,128]{3,1,2,0:T(8,128)}, bf16[9,512,2,128]{1,3,2...) while((s32[]{:T(128)}, f32[512,2,128]{0,2,1:T(8,128)S(1)}, ...), condition=%wide.region_11.0_spmd.clone, body=%wide.region_9.0_spmd.clone.sunk | while | flops 543687680 | bytes 12621060 | solution.py:160
  402.0 10.7 %collective-permute-start.24 = (f32[512,2,128]{2,0,1:T(8,128)S(1)}, f32[512,2,128]{2,0,1:T(8,128)S(1)}, u32[]{:S(2)}, u32[]{:S(2)}) collective-permute-start(f32[512,2,128]{2,0,1:T(8,128)S(1)} %get-tuple-element.906), channel_id=1, source_target_pairs={{8,0},{16,8},{24,16},{32,24},{40,32},{48,40},{56,48},{64,56},{72,6... | collective-permute-start | bytes 1572872 | tf_op jit(solution)/shard_map/ppermute | solution.py:17
  412.7 6.2 collective-permute-start.25
  418.8 5.6 collective-permute-start.26
  435.3 9.0 %collective-permute-done.25 = f32[512,2,128]{2,0,1:T(8,128)S(1)} collective-permute-done((f32[512,2,128]{2,0,1:T(8,128)S(1)}, f32[512,2,128]{2,0,1:T(8,128)S(1)}, u32[]{:S(2)}, u32[]{:S(2)}) %collective-permute-start.25) | collective-permute-done | bytes 524320 | tf_op jit(solution)/shard_map/ppermute | solution.py:17
  451.2 13.1 %collective-permute-start.16 = (f32[512,2,128]{2,0,1:T(8,128)S(1)}, f32[512,2,128]{2,0,1:T(8,128)S(1)}, u32[]{:S(2)}, u32[]{:S(2)}) collective-permute-start(f32[512,2,128]{2,0,1:T(8,128)S(1)} %get-tuple-element.914), channel_id=1, source_target_pairs={{8,0},{16,8},{24,16},{32,24},{40,32},{48,40},{56,48},{64,56},{72,6... | collective-permute-start | bytes 1572872 | tf_op jit(solution)/shard_map/ppermute | solution.py:17
  464.3 6.0 collective-permute-done.28
  470.3 15.6 %collective-permute-start.17 = (f32[512,2,128]{2,0,1:T(8,128)S(1)}, f32[512,2,128]{2,0,1:T(8,128)S(1)}, u32[]{:S(2)}, u32[]{:S(2)}) collective-permute-start(f32[512,2,128]{2,0,1:T(8,128)S(1)} %get-tuple-element.919), channel_id=1, source_target_pairs={{16,0},{24,8},{32,16},{40,24},{48,32},{56,40},{64,48},{72,56},{80,... | collective-permute-start | bytes 1572872 | tf_op jit(solution)/shard_map/ppermute | solution.py:17
  485.9 6.0 collective-permute-done.29
  495.8 21.3 %collective-permute-done.31 = f32[512,2,128]{2,0,1:T(8,128)S(1)} collective-permute-done((f32[512,2,128]{2,0,1:T(8,128)S(1)}, f32[512,2,128]{2,0,1:T(8,128)S(1)}, u32[]{:S(2)}, u32[]{:S(2)}) %collective-permute-start.31) | collective-permute-done | bytes 524320 | tf_op jit(solution)/shard_map/ppermute | solution.py:17
  517.2 25.3 %collective-permute-start.20 = (f32[512,2,128]{2,0,1:T(8,128)}, f32[512,2,128]{2,0,1:T(8,128)}, u32[]{:S(2)}, u32[]{:S(2)}) collective-permute-start(f32[512,2,128]{2,0,1:T(8,128)} %get-tuple-element.916), channel_id=1, source_target_pairs={{40,0},{48,8},{56,16},{64,24},{72,32},{80,40},{88,48},{96,56},{104... | collective-permute-start | bytes 1572872 | tf_op jit(solution)/shard_map/ppermute | solution.py:17
  542.5 7.3 %collective-permute-start.21 = (f32[512,2,128]{2,0,1:T(8,128)}, f32[512,2,128]{2,0,1:T(8,128)}, u32[]{:S(2)}, u32[]{:S(2)}) collective-permute-start(f32[512,2,128]{2,0,1:T(8,128)} %get-tuple-element.915), channel_id=1, source_target_pairs={{48,0},{56,8},{64,16},{72,24},{80,32},{88,40},{96,48},{104,56},{11... | collective-permute-start | bytes 1572872 | tf_op jit(solution)/shard_map/ppermute | solution.py:17
  551.7 4.4 collective-permute-start.23
  560.2 8.3 %collective-permute-done.20 = f32[512,2,128]{2,0,1:T(8,128)} collective-permute-done((f32[512,2,128]{2,0,1:T(8,128)}, f32[512,2,128]{2,0,1:T(8,128)}, u32[]{:S(2)}, u32[]{:S(2)}) %collective-permute-start.20) | collective-permute-done | bytes 524320 | tf_op jit(solution)/shard_map/ppermute | solution.py:17
  568.5 13.1 %collective-permute-done.21 = f32[512,2,128]{2,0,1:T(8,128)} collective-permute-done((f32[512,2,128]{2,0,1:T(8,128)}, f32[512,2,128]{2,0,1:T(8,128)}, u32[]{:S(2)}, u32[]{:S(2)}) %collective-permute-start.21) | collective-permute-done | bytes 524320 | tf_op jit(solution)/shard_map/ppermute | solution.py:17
  581.6 8.4 %collective-permute-done.22 = f32[512,2,128]{2,0,1:T(8,128)} collective-permute-done((f32[512,2,128]{2,0,1:T(8,128)}, f32[512,2,128]{2,0,1:T(8,128)}, u32[]{:S(2)}, u32[]{:S(2)}) %collective-permute-start.22) | collective-permute-done | bytes 524320 | tf_op jit(solution)/shard_map/ppermute | solution.py:17
  590.0 16.7 %collective-permute-done.23 = f32[512,2,128]{2,0,1:T(8,128)} collective-permute-done((f32[512,2,128]{2,0,1:T(8,128)}, f32[512,2,128]{2,0,1:T(8,128)}, u32[]{:S(2)}, u32[]{:S(2)}) %collective-permute-start.23) | collective-permute-done | bytes 524320 | tf_op jit(solution)/shard_map/ppermute | solution.py:17
  (391 shorter events, 353.5 us)
Async XLA Ops:
  7.2 267.4 %all-gather.2.cloned.1.call-start = ((), (), s32[]{:S(2)}) async-start(), calls=%async_computation.3 | async-start | bytes 4718592 | tf_op jit(solution)/shard_map/all_gather | solution.py:112
  8.5 22.4 %collective-permute-start = (bf16[512,256]{0,1:T(8,128)(2,1)S(1)}, bf16[512,256]{0,1:T(8,128)(2,1)}, u32[]{:S(2)}, u32[]{:S(2)}) collective-permute-start(bf16[512,256]{0,1:T(8,128)(2,1)S(1)} %copy.30), channel_id=1, source_target_pairs={{0,64},{8,72},{16,80},{24,88},{32,96},{40,104},{48,112},{56,120},{... | collective-permute-start | bytes 786440 | tf_op jit(solution)/shard_map/ppermute | solution.py:17
  11.7 30.6 %collective-permute-start.1 = (bf16[512,256]{0,1:T(8,128)(2,1)S(1)}, bf16[512,256]{0,1:T(8,128)(2,1)}, u32[]{:S(2)}, u32[]{:S(2)}) collective-permute-start(bf16[512,256]{0,1:T(8,128)(2,1)S(1)} %copy.30), channel_id=1, source_target_pairs={{0,56},{8,64},{16,72},{24,80},{32,88},{40,96},{48,104},{56,112},{6... | collective-permute-start | bytes 786440 | tf_op jit(solution)/shard_map/ppermute | solution.py:17
  13.6 42.4 %collective-permute-start.2 = (bf16[512,256]{0,1:T(8,128)(2,1)S(1)}, bf16[512,256]{0,1:T(8,128)(2,1)}, u32[]{:S(2)}, u32[]{:S(2)}) collective-permute-start(bf16[512,256]{0,1:T(8,128)(2,1)S(1)} %copy.30), channel_id=1, source_target_pairs={{0,48},{8,56},{16,64},{24,72},{32,80},{40,88},{48,96},{56,104},{64... | collective-permute-start | bytes 786440 | tf_op jit(solution)/shard_map/ppermute | solution.py:17
  15.5 44.1 %collective-permute-start.3 = (bf16[512,256]{0,1:T(8,128)(2,1)S(1)}, bf16[512,256]{0,1:T(8,128)(2,1)}, u32[]{:S(2)}, u32[]{:S(2)}) collective-permute-start(bf16[512,256]{0,1:T(8,128)(2,1)S(1)} %copy.30), channel_id=1, source_target_pairs={{0,40},{8,48},{16,56},{24,64},{32,72},{40,80},{48,88},{56,96},{64,... | collective-permute-start | bytes 786440 | tf_op jit(solution)/shard_map/ppermute | solution.py:17
  18.1 20.5 %collective-permute-start.8 = (bf16[512,256]{1,0:T(8,128)(2,1)}, bf16[512,256]{1,0:T(8,128)(2,1)}, u32[]{:S(2)}, u32[]{:S(2)}) collective-permute-start(bf16[512,256]{1,0:T(8,128)(2,1)} %param.20), channel_id=1, source_target_pairs={{0,64},{8,72},{16,80},{24,88},{32,96},{40,104},{48,112},{56,120},{... | collective-permute-start | bytes 786440 | tf_op jit(solution)/shard_map/ppermute | solution.py:17
  20.0 589.6 %reduce-scatter.3.cloned.1.call-start = ((), (), s32[]{:S(2)}) async-start(), calls=%async_computation.2 | async-start | bytes 9437184 | tf_op jit(solution)/shard_map/reduce_scatter | solution.py:109
  30.9 32.3 %collective-permute-start.4 = (bf16[512,256]{0,1:T(8,128)(2,1)S(1)}, bf16[512,256]{0,1:T(8,128)(2,1)}, u32[]{:S(2)}, u32[]{:S(2)}) collective-permute-start(bf16[512,256]{0,1:T(8,128)(2,1)S(1)} %copy.30), channel_id=1, source_target_pairs={{0,32},{8,40},{16,48},{24,56},{32,64},{40,72},{48,80},{56,88},{64,... | collective-permute-start | bytes 786440 | tf_op jit(solution)/shard_map/ppermute | solution.py:17
  38.5 28.3 %collective-permute-start.5 = (bf16[512,256]{0,1:T(8,128)(2,1)S(1)}, bf16[512,256]{0,1:T(8,128)(2,1)}, u32[]{:S(2)}, u32[]{:S(2)}) collective-permute-start(bf16[512,256]{0,1:T(8,128)(2,1)S(1)} %copy.30), channel_id=1, source_target_pairs={{0,24},{8,32},{16,40},{24,48},{32,56},{40,64},{48,72},{56,80},{64,... | collective-permute-start | bytes 786440 | tf_op jit(solution)/shard_map/ppermute | solution.py:17
  42.3 28.2 %collective-permute-start.6 = (bf16[512,256]{0,1:T(8,128)(2,1)S(1)}, bf16[512,256]{0,1:T(8,128)(2,1)S(1)}, u32[]{:S(2)}, u32[]{:S(2)}) collective-permute-start(bf16[512,256]{0,1:T(8,128)(2,1)S(1)} %copy.30), channel_id=1, source_target_pairs={{0,16},{8,24},{16,32},{24,40},{32,48},{40,56},{48,64},{56,72},{64,... | collective-permute-start | bytes 786440 | tf_op jit(solution)/shard_map/ppermute | solution.py:17
  56.0 17.5 %collective-permute-start.7 = (bf16[512,256]{0,1:T(8,128)(2,1)S(1)}, bf16[512,256]{0,1:T(8,128)(2,1)S(1)}, u32[]{:S(2)}, u32[]{:S(2)}) collective-permute-start(bf16[512,256]{0,1:T(8,128)(2,1)S(1)} %copy.30), channel_id=1, source_target_pairs={{0,8},{8,16},{16,24},{24,32},{32,40},{40,48},{48,56},{56,64},{64,7... | collective-permute-start | bytes 786440 | tf_op jit(solution)/shard_map/ppermute | solution.py:17
  59.6 17.3 %collective-permute-start.9 = (bf16[512,256]{1,0:T(8,128)(2,1)}, bf16[512,256]{1,0:T(8,128)(2,1)S(1)}, u32[]{:S(2)}, u32[]{:S(2)}) collective-permute-start(bf16[512,256]{1,0:T(8,128)(2,1)} %param.20), channel_id=1, source_target_pairs={{0,56},{8,64},{16,72},{24,80},{32,88},{40,96},{48,104},{56,112},{6... | collective-permute-start | bytes 786440 | tf_op jit(solution)/shard_map/ppermute | solution.py:17
  63.2 17.7 %collective-permute-start.10 = (bf16[512,256]{1,0:T(8,128)(2,1)}, bf16[512,256]{1,0:T(8,128)(2,1)}, u32[]{:S(2)}, u32[]{:S(2)}) collective-permute-start(bf16[512,256]{1,0:T(8,128)(2,1)} %param.20), channel_id=1, source_target_pairs={{0,48},{8,56},{16,64},{24,72},{32,80},{40,88},{48,96},{56,104},{64... | collective-permute-start | bytes 786440 | tf_op jit(solution)/shard_map/ppermute | solution.py:17
  66.8 19.4 %collective-permute-start.11 = (bf16[512,256]{1,0:T(8,128)(2,1)}, bf16[512,256]{1,0:T(8,128)(2,1)}, u32[]{:S(2)}, u32[]{:S(2)}) collective-permute-start(bf16[512,256]{1,0:T(8,128)(2,1)} %param.20), channel_id=1, source_target_pairs={{0,40},{8,48},{16,56},{24,64},{32,72},{40,80},{48,88},{56,96},{64,... | collective-permute-start | bytes 786440 | tf_op jit(solution)/shard_map/ppermute | solution.py:17
  81.0 18.4 %collective-permute-start.15 = (bf16[512,256]{1,0:T(8,128)(2,1)}, bf16[512,256]{1,0:T(8,128)(2,1)}, u32[]{:S(2)}, u32[]{:S(2)}) collective-permute-start(bf16[512,256]{1,0:T(8,128)(2,1)} %param.20), channel_id=1, source_target_pairs={{0,8},{8,16},{16,24},{24,32},{32,40},{40,48},{48,56},{56,64},{64,7... | collective-permute-start | bytes 786440 | tf_op jit(solution)/shard_map/ppermute | solution.py:17
  282.8 328.8 %reduce-scatter.5.cloned.1.call-start = ((), (), s32[]{:S(2)}) async-start(), calls=%async_computation.4 | async-start | bytes 4325376 | tf_op jit(solution)/shard_map/reduce_scatter | solution.py:121
  402.0 26.7 %collective-permute-start.24 = (f32[512,2,128]{2,0,1:T(8,128)S(1)}, f32[512,2,128]{2,0,1:T(8,128)S(1)}, u32[]{:S(2)}, u32[]{:S(2)}) collective-permute-start(f32[512,2,128]{2,0,1:T(8,128)S(1)} %get-tuple-element.906), channel_id=1, source_target_pairs={{8,0},{16,8},{24,16},{32,24},{40,32},{48,40},{56,48},{64,56},{72,6... | collective-permute-start | bytes 1572872 | tf_op jit(solution)/shard_map/ppermute | solution.py:17
  412.7 31.7 %collective-permute-start.25 = (f32[512,2,128]{2,0,1:T(8,128)S(1)}, f32[512,2,128]{2,0,1:T(8,128)S(1)}, u32[]{:S(2)}, u32[]{:S(2)}) collective-permute-start(f32[512,2,128]{2,0,1:T(8,128)S(1)} %get-tuple-element.911), channel_id=1, source_target_pairs={{16,0},{24,8},{32,16},{40,24},{48,32},{56,40},{64,48},{72,56},{80,... | collective-permute-start | bytes 1572872 | tf_op jit(solution)/shard_map/ppermute | solution.py:17
  418.8 28.3 %collective-permute-start.26 = (f32[512,2,128]{2,0,1:T(8,128)S(1)}, f32[512,2,128]{2,0,1:T(8,128)S(1)}, u32[]{:S(2)}, u32[]{:S(2)}) collective-permute-start(f32[512,2,128]{2,0,1:T(8,128)S(1)} %get-tuple-element.910), channel_id=1, source_target_pairs={{24,0},{32,8},{40,16},{48,24},{56,32},{64,40},{72,48},{80,56},{88,... | collective-permute-start | bytes 1572872 | tf_op jit(solution)/shard_map/ppermute | solution.py:17
  424.5 26.7 %collective-permute-start.27 = (f32[512,2,128]{2,0,1:T(8,128)S(1)}, f32[512,2,128]{2,0,1:T(8,128)S(1)}, u32[]{:S(2)}, u32[]{:S(2)}) collective-permute-start(f32[512,2,128]{2,0,1:T(8,128)S(1)} %get-tuple-element.909), channel_id=1, source_target_pairs={{32,0},{40,8},{48,16},{56,24},{64,32},{72,40},{80,48},{88,56},{96,... | collective-permute-start | bytes 1572872 | tf_op jit(solution)/shard_map/ppermute | solution.py:17
  426.8 43.5 %collective-permute-start.28 = (f32[512,2,128]{2,0,1:T(8,128)S(1)}, f32[512,2,128]{2,0,1:T(8,128)S(1)}, u32[]{:S(2)}, u32[]{:S(2)}) collective-permute-start(f32[512,2,128]{2,0,1:T(8,128)S(1)} %get-tuple-element.908), channel_id=1, source_target_pairs={{40,0},{48,8},{56,16},{64,24},{72,32},{80,40},{88,48},{96,56},{104... | collective-permute-start | bytes 1572872 | tf_op jit(solution)/shard_map/ppermute | solution.py:17
  428.7 63.2 %collective-permute-start.29 = (f32[512,2,128]{2,0,1:T(8,128)S(1)}, f32[512,2,128]{2,0,1:T(8,128)S(1)}, u32[]{:S(2)}, u32[]{:S(2)}) collective-permute-start(f32[512,2,128]{2,0,1:T(8,128)S(1)} %get-tuple-element.907), channel_id=1, source_target_pairs={{48,0},{56,8},{64,16},{72,24},{80,32},{88,40},{96,48},{104,56},{11... | collective-permute-start | bytes 1572872 | tf_op jit(solution)/shard_map/ppermute | solution.py:17
  444.3 49.5 %collective-permute-start.30 = (f32[512,2,128]{2,0,1:T(8,128)S(1)}, f32[512,2,128]{2,0,1:T(8,128)S(1)}, u32[]{:S(2)}, u32[]{:S(2)}) collective-permute-start(f32[512,2,128]{2,0,1:T(8,128)S(1)} %get-tuple-element.913), channel_id=1, source_target_pairs={{56,0},{64,8},{72,16},{80,24},{88,32},{96,40},{104,48},{112,56},{1... | collective-permute-start | bytes 1572872 | tf_op jit(solution)/shard_map/ppermute | solution.py:17
  447.2 70.0 %collective-permute-start.31 = (f32[512,2,128]{2,0,1:T(8,128)S(1)}, f32[512,2,128]{2,0,1:T(8,128)S(1)}, u32[]{:S(2)}, u32[]{:S(2)}) collective-permute-start(f32[512,2,128]{2,0,1:T(8,128)S(1)} %get-tuple-element.912), channel_id=1, source_target_pairs={{64,0},{72,8},{80,16},{88,24},{96,32},{104,40},{112,48},{120,56},{... | collective-permute-start | bytes 1572872 | tf_op jit(solution)/shard_map/ppermute | solution.py:17
  451.2 91.2 %collective-permute-start.16 = (f32[512,2,128]{2,0,1:T(8,128)S(1)}, f32[512,2,128]{2,0,1:T(8,128)S(1)}, u32[]{:S(2)}, u32[]{:S(2)}) collective-permute-start(f32[512,2,128]{2,0,1:T(8,128)S(1)} %get-tuple-element.914), channel_id=1, source_target_pairs={{8,0},{16,8},{24,16},{32,24},{40,32},{48,40},{56,48},{64,56},{72,6... | collective-permute-start | bytes 1572872 | tf_op jit(solution)/shard_map/ppermute | solution.py:17
  470.3 79.5 %collective-permute-start.17 = (f32[512,2,128]{2,0,1:T(8,128)S(1)}, f32[512,2,128]{2,0,1:T(8,128)S(1)}, u32[]{:S(2)}, u32[]{:S(2)}) collective-permute-start(f32[512,2,128]{2,0,1:T(8,128)S(1)} %get-tuple-element.919), channel_id=1, source_target_pairs={{16,0},{24,8},{32,16},{40,24},{48,32},{56,40},{64,48},{72,56},{80,... | collective-permute-start | bytes 1572872 | tf_op jit(solution)/shard_map/ppermute | solution.py:17
  492.0 59.7 %collective-permute-start.18 = (f32[512,2,128]{2,0,1:T(8,128)S(1)}, f32[512,2,128]{2,0,1:T(8,128)S(1)}, u32[]{:S(2)}, u32[]{:S(2)}) collective-permute-start(f32[512,2,128]{2,0,1:T(8,128)S(1)} %get-tuple-element.918), channel_id=1, source_target_pairs={{24,0},{32,8},{40,16},{48,24},{56,32},{64,40},{72,48},{80,56},{88,... | collective-permute-start | bytes 1572872 | tf_op jit(solution)/shard_map/ppermute | solution.py:17
  493.9 66.3 %collective-permute-start.19 = (f32[512,2,128]{2,0,1:T(8,128)}, f32[512,2,128]{2,0,1:T(8,128)}, u32[]{:S(2)}, u32[]{:S(2)}) collective-permute-start(f32[512,2,128]{2,0,1:T(8,128)} %get-tuple-element.917), channel_id=1, source_target_pairs={{32,0},{40,8},{48,16},{56,24},{64,32},{72,40},{80,48},{88,56},{96,... | collective-permute-start | bytes 1572872 | tf_op jit(solution)/shard_map/ppermute | solution.py:17
  517.2 51.3 %collective-permute-start.20 = (f32[512,2,128]{2,0,1:T(8,128)}, f32[512,2,128]{2,0,1:T(8,128)}, u32[]{:S(2)}, u32[]{:S(2)}) collective-permute-start(f32[512,2,128]{2,0,1:T(8,128)} %get-tuple-element.916), channel_id=1, source_target_pairs={{40,0},{48,8},{56,16},{64,24},{72,32},{80,40},{88,48},{96,56},{104... | collective-permute-start | bytes 1572872 | tf_op jit(solution)/shard_map/ppermute | solution.py:17
  542.5 39.1 %collective-permute-start.21 = (f32[512,2,128]{2,0,1:T(8,128)}, f32[512,2,128]{2,0,1:T(8,128)}, u32[]{:S(2)}, u32[]{:S(2)}) collective-permute-start(f32[512,2,128]{2,0,1:T(8,128)} %get-tuple-element.915), channel_id=1, source_target_pairs={{48,0},{56,8},{64,16},{72,24},{80,32},{88,40},{96,48},{104,56},{11... | collective-permute-start | bytes 1572872 | tf_op jit(solution)/shard_map/ppermute | solution.py:17
  549.8 40.2 %collective-permute-start.22 = (f32[512,2,128]{2,0,1:T(8,128)}, f32[512,2,128]{2,0,1:T(8,128)}, u32[]{:S(2)}, u32[]{:S(2)}) collective-permute-start(f32[512,2,128]{2,0,1:T(8,128)} %get-tuple-element.921), channel_id=1, source_target_pairs={{56,0},{64,8},{72,16},{80,24},{88,32},{96,40},{104,48},{112,56},{1... | collective-permute-start | bytes 1572872 | tf_op jit(solution)/shard_map/ppermute | solution.py:17
  551.7 55.0 %collective-permute-start.23 = (f32[512,2,128]{2,0,1:T(8,128)}, f32[512,2,128]{2,0,1:T(8,128)}, u32[]{:S(2)}, u32[]{:S(2)}) collective-permute-start(f32[512,2,128]{2,0,1:T(8,128)} %get-tuple-element.920), channel_id=1, source_target_pairs={{64,0},{72,8},{80,16},{88,24},{96,32},{104,40},{112,48},{120,56},{... | collective-permute-start | bytes 1572872 | tf_op jit(solution)/shard_map/ppermute | solution.py:17
  (29 other events, 1114.7 us)
Sparse Core Ops, SparseCore 0:
  20.1 55.9 all-gather.1
  283.0 108.6 reduce-scatter.2
  396.1 195.4 reduce-scatter.4
where the time goes:
time: 623 us; the launch traced here: 618 us
  starting transfers between devices  154 us (25%)
  matrix products  144 us (23%)
  local copies, waits for them, and re-layouts  111 us (18%)
  waiting for transfers between devices  104 us (17%)
  other arithmetic  88.9 us (14%)
  between operations  14.4 us (2%)
    ppermute x32, starting transfers between devices, shifted_2(): return lax.ppermute(value, axis, pairs)  154 us
    ppermute x32, waiting for transfers between devices, shifted_2(): return lax.ppermute(value, axis, pairs)  104 us
    dynamic_slice x18, local copies, waits for them, and re-layouts, block_probs(): scores = score_store[block_index]  54.3 us
    scatter x9, other arithmetic, stats_step(): return (new_max, new_sum, score_store.at[block_index].set(scores))  36.6 us
    dot_general x9, matrix products, grad_step(): jnp.einsum('htk,thd->khd', probs_low, grad_heads, preferred_element_type=...  32.7 us
    dot_general x9, matrix products, grad_step(): jnp.einsum('htk,thd->khd', grad_scores, query_heads, preferred_element_ty...  26.5 us
    dot_general x9, matrix products, grad_step(): jnp.einsum('thd,khd->htk', grad_heads, values_block, preferred_element_ty...  23.4 us
    unnamed x55, local copies, waits for them, and re-layouts  22.5 us
  transfers between devices with their start and end apart: 35, of which 13 were waited for; matrix products, arithmetic and copies ran while one was open for 54% of the time, Pallas kernels for 0%

commit v1 on v0

v1 whole, which is shorter than its diff:
```python
import functools
import math

import jax
import jax.numpy as jnp
from jax import lax
from jax.experimental import pallas as pl
from jax.experimental.pallas import tpu as pltpu
from jax.sharding import PartitionSpec as P

HD = 128
T = 512
CT = 1024
SUB = 256
REACH = 4
DOCS = 24
TOOLS = 16
LSE_ROW = DOCS + TOOLS
MASK = 131072.0
SCALE = 1.0 / math.sqrt(HD)
LOG2 = SCALE * math.log2(math.e)
MESH = pl.DeviceIdType.MESH
F32 = jnp.float32
BF16 = jnp.bfloat16


def dot(a, b):
    return jnp.dot(a, b, preferred_element_type=F32)


def dot_tn(a, b):
    return lax.dot_general(a, b, (((0,), (0,)), ((), ())), preferred_element_type=F32)


def dot_nt(a, b):
    return lax.dot_general(a, b, (((1,), (1,)), ((), ())), preferred_element_type=F32)


def thirds(x):
    high = x.astype(BF16)
    rest = x - high.astype(F32)
    mid = rest.astype(BF16)
    return high.astype(F32), mid.astype(F32), (rest - mid.astype(F32))


def kernel(
    nc, nz,
    seg, tool, q_in, k_in, v_in, w_in, gm_in,
    out, dq_out, dk_out, dv_out, gw_out,
    qs, kv, fk, qt, m_s, l_s, ot, otb, ob, gmf, da, dos, dob, dotr, dqt, wsl, atf, lo,
    d0, sa, sb, s4, ra, rb, rf, rf4, fin, pg, gown, gws, gwr, gsum, gwi,
    swap_s, swap_r, kv_s, kv_r, zg_s, zg_r, za_s, za_r, w1_s, w1_r, w2_s, w2_r,
    w3_s, w3_r, at_s, at_r, do_s, do_r, ch_s, ch_r, fn_s, fn_r, gx_s, gx_r, gw_s, gw_r,
):
    me = lax.axis_index("ctx")
    z = lax.axis_index("head")
    m = me // 2
    c = lax.rem(me, 2)
    o = 1 - c
    sib = me + 1 - 2 * c

    def chip(by):
        return lax.rem(m + by + nc, nc)

    def at_chip(by):
        return 2 * chip(by) + c

    def zed(by):
        return lax.rem(z + by + nz, nz)

    def remote(src, dst, ss, rs, ctx, head):
        return pltpu.make_async_remote_copy(
            src_ref=src, dst_ref=dst, send_sem=ss, recv_sem=rs,
            device_id=(ctx, head), device_id_type=MESH,
        )

    def cols(index, width):
        return pl.ds(pl.multiple_of(index * width, width), width)

    sent = []

    def start(copy):
        copy.start()
        sent.append(copy)

    barrier = pltpu.get_barrier_semaphore()
    pl.semaphore_signal(barrier, inc=1, device_id=(sib, z), device_id_type=MESH)

    @pl.loop(1, nc)
    def _(by):
        pl.semaphore_signal(barrier, inc=1, device_id=(at_chip(by), z), device_id_type=MESH)

    @pl.loop(1, nz)
    def _(by):
        pl.semaphore_signal(barrier, inc=1, device_id=(me, zed(by)), device_id_type=MESH)

    pl.semaphore_wait(barrier, 1 + (nc - 1) + (nz - 1))

    for t, (src, dst) in enumerate(((q_in, qs.at[c]), (k_in, kv.at[0, c, 0]), (v_in, kv.at[0, c, 1]))):
        start(remote(src.at[:, cols(o, HD)], dst, swap_s.at[t], swap_r.at[t], sib, z))

    full = nz // 2 - 1

    def ring_has(step, half, right):
        return step <= full or (step == full + 1 and half == (0 if right else 1))

    def ring_send(buf, ss, rs, step, half, src=None):
        for side, right in enumerate((True, False)):
            if ring_has(step, half, right):
                block = zed(1 - step) if right else zed(step - 1)
                to = zed(1) if right else zed(-1)
                k = side * 8 + (step - 1) * 2 + half
                dst = buf.at[block, half]
                start(remote(dst if src is None else src, dst, ss.at[k], rs.at[k], me, to))

    def ring_recv(buf, ss, rs, step, half):
        for side, right in enumerate((True, False)):
            if ring_has(step, half, right):
                block = zed(-step) if right else zed(step)
                k = side * 8 + (step - 1) * 2 + half
                dst = buf.at[block, half]
                remote(dst, dst, ss.at[k], rs.at[k], me, z).wait_recv()

    for half in range(2):
        ring_send(gmf, zg_s, zg_r, 1, half, gm_in.at[half])

    rows16 = pl.ds(pl.multiple_of(m * 16, 16), 16)
    wide = cols(c, SUB)

    @pl.loop(1, nz)
    def _(by):
        to = zed(by)
        src = w_in.at[rows16, pl.ds(pl.multiple_of(to * T + c * SUB, SUB), SUB)]
        remote(src, wsl.at[z, rows16, wide], w1_s.at[by], w1_r.at[by], me, to).start()

    wsl[z, rows16, wide] = w_in[rows16, pl.ds(pl.multiple_of(z * T + c * SUB, SUB), SUB)]

    gmf[z] = gm_in[...]
    qs[c] = q_in[:, cols(c, HD)]
    kv[0, c, 0] = k_in[:, cols(c, HD)]
    kv[0, c, 1] = v_in[:, cols(c, HD)]

    row = lax.broadcasted_iota(jnp.int32, (HD, CT), 0)
    pos = lax.broadcasted_iota(jnp.int32, (HD, CT), 1)
    block64 = lax.shift_right_logical(pos, 6)
    is_doc = row < DOCS
    is_tool = (row >= DOCS) & (row < LSE_ROW)
    for d in range(REACH + 1):
        seg_row = seg[pl.ds(chip(-d), 1), :]
        tool_row = tool[pl.ds(chip(-d), 1), :]
        if d == 0:
            bad_tool = (block64 > row - DOCS) | ((tool_row != 0) & (block64 != row - DOCS))
        else:
            bad_tool = jnp.broadcast_to(tool_row != 0, row.shape)
        bad = (is_doc & (seg_row != row)) | (is_tool & bad_tool)
        feat = jnp.where(bad, -MASK, jnp.where((row >= LSE_ROW) & (row < LSE_ROW + 3), -1.0, 0.0))
        fk[d] = feat.T.astype(BF16)
    seg_row = seg[pl.ds(m, 1), :]
    hot = (is_doc & (seg_row == row)) | (is_tool & (block64 == row - DOCS))
    qfeat = jnp.where(hot, 1.0, 0.0)
    qt[HD:, :] = qfeat.astype(BF16)

    for t, dst in enumerate((qs.at[o], kv.at[0, o, 0], kv.at[0, o, 1])):
        remote(dst, dst, swap_s.at[t], swap_r.at[t], sib, z).wait_recv()

    kv_moves = {
        (1, 0): (0, 1), (3, 1): (0, 3), (4, 0): (0, 4), (4, 1): (0, 4),
        (2, 0): (1, 1), (3, 0): (2, 1), (2, 1): (3, -1), (1, 1): (2, -1),
    }
    kv_key = {key: index for index, key in enumerate(kv_moves)}

    def kv_send(key):
        source, by = kv_moves[key]
        k = kv_key[key]
        start(remote(kv.at[source, key[1]], kv.at[key], kv_s.at[k], kv_r.at[k], at_chip(by), z))

    def kv_recv(key):
        k = kv_key[key]
        remote(kv.at[key], kv.at[key], kv_s.at[k], kv_r.at[k], me, z).wait_recv()

    for key in ((1, 0), (3, 1), (4, 0), (4, 1)):
        kv_send(key)

    qt[:HD, :] = jnp.concatenate([qs[0].astype(F32).T, qs[1].astype(F32).T], axis=1).astype(BF16)
    m_s[...] = jnp.full(m_s.shape, -1e30, F32)
    l_s[...] = jnp.zeros(l_s.shape, F32)
    ot[...] = jnp.zeros(ot.shape, F32)
    da[...] = jnp.zeros(da.shape, F32)

    def span(key):
        if key == (0, 1):
            return T, T
        if key == (REACH, 0):
            return 0, T
        return 0, CT

    def scores(key, sub):
        d, h = key
        q0, qn = span(key)
        rows = pl.ds(pl.multiple_of(sub * SUB, SUB), SUB)
        frows = pl.ds(pl.multiple_of(h * T + sub * SUB, SUB), SUB)
        k_tile = kv[d, h, 0, rows, :]
        s = dot(jnp.concatenate([k_tile, fk[d, frows, :]], axis=1), qt[:, q0:q0 + qn])
        if d == 0:
            key_pos = h * T + sub * SUB + lax.broadcasted_iota(jnp.int32, s.shape, 0)
            query_pos = q0 + lax.broadcasted_iota(jnp.int32, s.shape, 1)
            s = jnp.where(key_pos <= query_pos, s, -2.0 * MASK)
        return s, k_tile, kv[d, h, 1, rows, :]

    def forward(key):
        q0, qn = span(key)

        @pl.loop(0, T // SUB)
        def _(sub):
            s, _, v_tile = scores(key, sub)
            old = m_s[:, q0:q0 + qn]
            new = jnp.maximum(old, jnp.max(s, axis=0, keepdims=True))
            p = jnp.exp2((s - new) * LOG2)
            fade = jnp.exp2((old - new) * LOG2)
            m_s[:, q0:q0 + qn] = new
            l_s[:, q0:q0 + qn] = l_s[:, q0:q0 + qn] * fade + jnp.sum(p, axis=0, keepdims=True)
            ot[:, q0:q0 + qn] = ot[:, q0:q0 + qn] * fade + dot_tn(v_tile, p.astype(BF16))

    def grad_block(block):
        w_cols = w_in[:, pl.ds(pl.multiple_of(block * T, T), T)]
        for half in range(2):
            rows = slice(half * SUB, half * SUB + SUB)
            da[rows, :] = da[rows, :] + dot_nt(gmf[block, half], w_cols)

    def gm_step(k):
        step, half = k // 2 + 1, k % 2
        ring_recv(gmf, zg_s, zg_r, step, half)
        ring_send(gmf, zg_s, zg_r, step + 1, half)

    def kv_step(key, then=None):
        kv_recv(key)
        if then is not None:
            kv_send(then)

    forward((0, 0))
    forward((0, 1))
    kv_step((1, 0), (2, 0))
    gm_step(0)
    forward((1, 0))
    kv_step((3, 1), (2, 1))
    grad_block(z)
    forward((3, 1))
    kv_step((2, 0), (3, 0))
    gm_step(1)
    forward((2, 0))
    kv_step((2, 1), (1, 1))
    forward((2, 1))
    kv_recv((4, 0))
    forward((4, 0))
    grad_block(zed(1))
    grad_block(zed(-1))
    gm_step(2)
    kv_recv((3, 0))
    forward((3, 0))
    kv_recv((4, 1))
    forward((4, 1))

    @pl.loop(1, nz)
    def _(by):
        src = wsl.at[zed(-by), rows16, wide]
        remote(src, src, w1_s.at[by], w1_r.at[by], me, z).wait_recv()

    gm_step(3)
    kv_recv((1, 1))
    forward((1, 1))

    @pl.loop(1, nc)
    def _(by):
        src = wsl.at[:, rows16, wide]
        remote(src, src, w2_s.at[by], w2_r.at[by], at_chip(by), z).start()

    inv = 1.0 / l_s[...]
    lse = m_s[...] + jnp.log2(l_s[...]) * (1.0 / LOG2)
    att = ot[...] * inv
    otb[...] = att.astype(BF16)
    for h in range(2):
        ob[h] = att[:, h * T:(h + 1) * T].T.astype(BF16).reshape(2, SUB, HD)
    mine = cols(c, HD)
    start(remote(ob.at[o], atf.at[z, :, :, mine], at_s, at_r, sib, z))
    atf[z, :, :, mine] = ob[c]
    high, mid, low = thirds(lse)
    qt[HD:, :] = jnp.where(
        row == LSE_ROW, high,
        jnp.where(row == LSE_ROW + 1, mid, jnp.where(row == LSE_ROW + 2, low, qfeat)),
    ).astype(BF16)
    dst = atf.at[z, :, :, cols(o, HD)]
    remote(dst, dst, at_s, at_r, sib, z).wait_recv()

    def weight_block(block):
        part = dot_tn(atf[z, 0], gmf[block, 0]) + dot_tn(atf[z, 1], gmf[block, 1])
        pg[...] = part
        per = nc // nz
        for e in range(per):
            gown[block * per + e] = pg[:, pl.ds(pl.multiple_of(e * SUB + c * HD, HD), HD)]
            gws[block * per + e] = pg[:, pl.ds(pl.multiple_of(e * SUB + o * HD, HD), HD)].astype(BF16)

    grad_block(zed(2))
    grad_block(zed(-2))
    for by in (0, 1, -1, 2, -2):
        weight_block(zed(by))
    gm_step(4)
    gm_step(5)
    for half in range(2):
        ring_send(atf, za_s, za_r, 1, half)
    for by in (3, -3):
        grad_block(zed(by))
        weight_block(zed(by))
    gm_step(6)
    gm_step(7)
    grad_block(zed(4))

    dos[...] = da[:, cols(o, HD)].astype(BF16)
    start(remote(dos, dob.at[c], do_s, do_r, sib, z))
    dob[c] = da[:, mine].astype(BF16)

    weight_block(zed(4))
    start(remote(gws, gwr, gx_s, gx_r, sib, z))

    remote(dob.at[o], dob.at[o], do_s, do_r, sib, z).wait_recv()
    dot_rows = jnp.concatenate([dob[0].astype(F32).T, dob[1].astype(F32).T], axis=1)
    dotr[:HD, :] = dot_rows.astype(BF16)
    delta = jnp.sum(dot_rows * otb[...].astype(F32), axis=0, keepdims=True)
    high, mid, low = thirds(delta)
    dotr[HD:, :] = jnp.where(
        row == 0, high, jnp.where(row == 1, mid, jnp.where(row == 2, low, 0.0))
    ).astype(BF16)
    dqt[...] = jnp.zeros(dqt.shape, F32)
    minus = jnp.where(lax.broadcasted_iota(jnp.int32, (SUB, HD), 1) < 3, -1.0, 0.0).astype(BF16)

    def backward(key, finish):
        q0, qn = span(key)

        @pl.loop(0, T // SUB)
        def _(sub):
            rows = pl.ds(pl.multiple_of(sub * SUB, SUB), SUB)
            s, k_tile, v_tile = scores(key, sub)
            p = jnp.exp2(s * LOG2)
            dp = dot(jnp.concatenate([v_tile, minus], axis=1), dotr[:, q0:q0 + qn])
            ds = (p * dp).astype(BF16)
            if qn == CT:
                do_rows = dob[...].reshape(CT, HD)
                q_rows = qs[...].reshape(CT, HD)
            else:
                do_rows = dob[q0 // T]
                q_rows = qs[q0 // T]
            finish(rows, dot(ds, q_rows) * SCALE, dot(p.astype(BF16), do_rows))
            dqt[:, q0:q0 + qn] = dqt[:, q0:q0 + qn] + dot_tn(k_tile, ds)

    def keep(buf, *slot):
        def finish(rows, dk, dv):
            buf[(*slot, 0, rows)] = dk.astype(buf.dtype)
            buf[(*slot, 1, rows)] = dv.astype(buf.dtype)
        return finish

    def add_keep(buf, other, *slot):
        def finish(rows, dk, dv):
            buf[(*slot, 0, rows)] = (dk + other[(*slot, 0, rows)].astype(F32)).astype(BF16)
            buf[(*slot, 1, rows)] = (dv + other[(*slot, 1, rows)].astype(F32)).astype(BF16)
        return finish

    def att_step(k):
        step, half = k // 2 + 1, k % 2
        ring_recv(atf, za_s, za_r, step, half)
        ring_send(atf, za_s, za_r, step + 1, half)

    def stage(s):
        a, b = (s, 0), (REACH - s, 1)
        if s == 1:
            backward(a, keep(sa, 0))
        else:
            remote(ra.at[s - 1], ra.at[s - 1], ch_s.at[s - 2], ch_r.at[s - 2], me, z).wait_recv()
            backward(a, add_keep(sa, ra, s - 1))
        if s < REACH - 1:
            start(remote(sa.at[s - 1], ra.at[s], ch_s.at[s - 1], ch_r.at[s - 1], at_chip(1), z))
        else:
            start(remote(sa.at[s - 1], rf.at[0], ch_s.at[s - 1], ch_r.at[s - 1], at_chip(-3), z))
        if s == 1:
            backward(b, keep(sb, 0))
        else:
            remote(rb.at[s - 1], rb.at[s - 1], ch_s.at[s + 1], ch_r.at[s + 1], me, z).wait_recv()
            backward(b, add_keep(sb, rb, s - 1))
        if s < REACH - 1:
            start(remote(sb.at[s - 1], rb.at[s], ch_s.at[s + 2], ch_r.at[s + 2], at_chip(-1), z))
        else:
            start(remote(sb.at[s - 1], rf.at[1], ch_s.at[s + 2], ch_r.at[s + 2], at_chip(-1), z))

    stage(1)
    att_step(0)

    remote(gwr, gwr, gx_s, gx_r, sib, z).wait_recv()

    @pl.loop(1, nc)
    def _(by):
        to = lax.rem(m + by, nc)
        gsum[to] = (gown[to] + gwr[to].astype(F32)).astype(BF16)
        remote(gsum.at[to], gwi.at[by], gw_s.at[by], gw_r.at[by], at_chip(by), z).start()

    att_step(1)
    for h in range(2):
        backward((REACH, h), keep(s4, h))
    start(remote(s4, rf4, ch_s.at[6], ch_r.at[6], at_chip(-4), z))
    att_step(2)
    stage(2)
    att_step(3)
    for h in range(2):
        backward((0, h), keep(d0, h))

    @pl.loop(1, nc)
    def _(by):
        src = wsl.at[:, pl.ds(pl.multiple_of(chip(-by) * 16, 16), 16), wide]
        remote(src, src, w2_s.at[by], w2_r.at[by], me, z).wait_recv()

    start(remote(wsl.at[:, :, wide], wsl.at[:, :, wide], w3_s, w3_r, sib, z))
    att_step(4)
    att_step(5)
    stage(3)

    fin[0, 0] = (dqt[:, :T] * SCALE).T.astype(BF16)
    fin[0, 1] = (dqt[:, T:] * SCALE).T.astype(BF16)
    outs = (dq_out, dk_out, dv_out)
    start(remote(fin.at[0, o], dq_out.at[:, mine], fn_s.at[0], fn_r.at[0], sib, z))
    dq_out[:, mine] = fin[0, c]

    other = wsl.at[:, :, cols(o, SUB)]
    remote(other, other, w3_s, w3_r, sib, z).wait_recv()

    def out_block(block, first=False):
        for half in range(2):
            rows = slice(half * SUB, half * SUB + SUB)
            part = dot(atf[block, half], wsl[block])
            lo[rows, :] = part if first else lo[rows, :] + part

    out_block(z, True)
    for by in (1, -1, 2, -2, 3, -3):
        out_block(zed(by))

    total = gown[m] + gwr[m].astype(F32)
    for by in range(1, nc):
        remote(gwi.at[by], gwi.at[by], gw_s.at[by], gw_r.at[by], me, z).wait_recv()
        total = total + gwi[by].astype(F32)
    gw_out[...] = total

    att_step(6)
    att_step(7)
    out_block(zed(4))
    out[...] = lo[...].astype(BF16)

    remote(rf4, rf4, ch_s.at[6], ch_r.at[6], me, z).wait_recv()
    for h in range(2):
        remote(rf.at[h], rf.at[h], ch_s.at[2 + 3 * h], ch_r.at[2 + 3 * h], me, z).wait_recv()
        for t in range(2):
            fin[1 + t, h] = (d0[h, t] + rf[h, t].astype(F32) + rf4[h, t].astype(F32)).astype(BF16)
    for t in (1, 2):
        start(remote(fin.at[t, o], outs[t].at[:, mine], fn_s.at[t], fn_r.at[t], sib, z))
        outs[t][:, mine] = fin[t, c]
    for t in range(3):
        dst = outs[t].at[:, cols(o, HD)]
        remote(dst, dst, fn_s.at[t], fn_r.at[t], sib, z).wait_recv()

    for copy in sent:
        copy.wait_send()

    @pl.loop(1, nz)
    def _(by):
        src = wsl.at[z, rows16, wide]
        remote(src, src, w1_s.at[by], w1_r.at[by], me, zed(by)).wait_send()

    @pl.loop(1, nc)
    def _(by):
        src = wsl.at[:, rows16, wide]
        remote(src, src, w2_s.at[by], w2_r.at[by], at_chip(by), z).wait_send()
        remote(gwi.at[by], gwi.at[by], gw_s.at[by], gw_r.at[by], at_chip(by), z).wait_send()


def body(nc, nz, queries, key_in, values, segment, tool_ids, out_weight, grad_mixed):
    width = out_weight.shape[1]
    vm = pltpu.VMEM
    dma = pltpu.SemaphoreType.DMA
    one = dma(())
    grads = (2, T, HD)
    scratch = [
        vm((2, T, HD), BF16),
        vm((REACH + 1, 2, 2, T, HD), BF16),
        vm((REACH + 1, CT, HD), BF16),
        vm((2 * HD, CT), BF16),
        vm((1, CT), F32), vm((1, CT), F32),
        vm((HD, CT), F32),
        vm((HD, CT), BF16),
        vm((2, 2, SUB, HD), BF16),
        vm((nz, 2, SUB, T), BF16),
        vm((T, 2 * HD), F32),
        vm((T, HD), BF16),
        vm((2, T, HD), BF16),
        vm((2 * HD, CT), BF16),
        vm((HD, CT), F32),
        vm((nz, 2 * HD, T), BF16),
        vm((nz, 2, SUB, 2 * HD), BF16),
        vm((T, T), F32),
        vm((2, *grads), F32),
        vm((3, *grads), BF16), vm((3, *grads), BF16),
        vm((2, *grads), BF16),
        vm((3, *grads), BF16), vm((3, *grads), BF16),
        vm((2, *grads), BF16), vm((2, *grads), BF16),
        vm((3, 2, T, HD), BF16),
        vm((2 * HD, T), F32),
        vm((nc, 2 * HD, HD), F32),
        vm((nc, 2 * HD, HD), BF16), vm((nc, 2 * HD, HD), BF16),
        vm((nc, 2 * HD, HD), BF16), vm((nc, 2 * HD, HD), BF16),
        dma((3,)), dma((3,)),
        dma((8,)), dma((8,)),
        dma((16,)), dma((16,)), dma((16,)), dma((16,)),
        dma((nz,)), dma((nz,)), dma((nc,)), dma((nc,)), one, one,
        one, one, one, one,
        dma((7,)), dma((7,)), dma((3,)), dma((3,)),
        one, one, dma((nc,)), dma((nc,)),
    ]
    return pl.pallas_call(
        functools.partial(kernel, nc, nz),
        out_shape=(
            jax.ShapeDtypeStruct((T, width // nz), BF16),
            jax.ShapeDtypeStruct(queries.shape, BF16),
            jax.ShapeDtypeStruct(queries.shape, BF16),
            jax.ShapeDtypeStruct(queries.shape, BF16),
            jax.ShapeDtypeStruct((2 * HD, width // (2 * nc)), F32),
        ),
        in_specs=[pl.BlockSpec(memory_space=pltpu.VMEM)] * 7,
        out_specs=[pl.BlockSpec(memory_space=pltpu.VMEM)] * 5,
        scratch_shapes=scratch,
        compiler_params=pltpu.CompilerParams(
            collective_id=0, has_side_effects=True, vmem_limit_bytes=58 * 1024 * 1024
        ),
        cost_estimate=pl.CostEstimate(
            flops=20_000_000_000, bytes_accessed=8_000_000, transcendentals=10_000_000
        ),
    )(
        segment.reshape(nc, CT), tool_ids.reshape(nc, CT),
        queries, key_in, values, out_weight, grad_mixed.reshape(2, SUB, width // nz),
    )


def solution(mesh):
    nc, nz = mesh.shape["ctx"] // 2, mesh.shape["head"]
    split = P("ctx", "head")
    return jax.shard_map(
        functools.partial(body, nc, nz),
        mesh=mesh,
        in_specs=(split, split, split, P(), P(), P("head", None), split),
        out_specs=(split, split, split, split, P("head", "ctx")),
        check_vma=False,
    )
```

time: 623 us -> 129 us (0.21)
  the two profiles are of different devices: /device:TPU:244 before, /device:TPU:1 now
where the time goes in v1:
time: 129 us
  Pallas kernels  118 us (91%)
  local copies, waits for them, and re-layouts  9.59 us (7%)
    pallas_call x1, Pallas kernels, body(): pl.pallas_call(functools.partial(kernel, nc, nz), out_shape=(jax.ShapeDty...  118 us
    unnamed x9, local copies, waits for them, and re-layouts  6.62 us

profile of v1, /device:TPU:1, one launch (start us, length us, event | category | flops | bytes accessed | tf_op | source)
XLA Modules:
  0.0 128.7 jit_solution(17854789744888933107)
XLA Ops:
  0.6 1.5 %reshape.19.seg = s32[16,1024]{1,0:T(8,128)} reshape(s32[16384]{0:T(1024)} %param.10) | data formatting | bytes 131072 | tf_op jit(solution)/shard_map/reshape | solution.py:541
  2.1 1.5 %reshape.20.tool = s32[16,1024]{1,0:T(8,128)} reshape(s32[16384]{0:T(1024)} %param.11) | data formatting | bytes 131072 | tf_op jit(solution)/shard_map/reshape | solution.py:541
  3.6 118.5 %shard_map.110 = (bf16[512,512]{1,0:T(8,128)(2,1)}, bf16[512,256]{1,0:T(8,128)(2,1)}, bf16[512,256]{1,0:T(8,128)(2,1)}, bf16[512,256]{1,0:T(8,128)(2,1)}, f32[256,128]{1,0:T(8,128)}) custom-call(s32[16,1024]{1,0:T(8,128)} %reshape.19.seg, s32[16,1024]{1,0:T(8,128)} %reshape.20.tool, bf16[512,256]{1,0:T(8,128)(2,1)} %q_in.1, bf16[512,256]{1,0:T(8,128)(2,1)} %k_in.1, ...), custom_call_target="tpu_custom_call" | custom-call | flops 20000000000 | bytes 8000000 | tf_op jit(solution)/shard_map/pallas_call | solution.py:522
  122.1 0.0 copy-start
  122.1 0.0 copy-start.1
  122.1 1.9 %copy.17 = bf16[512,512]{1,0:T(8,128)(2,1)} copy(bf16[512,512]{1,0:T(8,128)(2,1)} %get-tuple-element.10) | data formatting | bytes 1048576
  124.0 1.7 %copy.18 = bf16[512,256]{1,0:T(8,128)(2,1)} copy(bf16[512,256]{1,0:T(8,128)(2,1)} %get-tuple-element.11) | data formatting | bytes 524288
  125.7 1.7 %copy.19 = bf16[512,256]{1,0:T(8,128)(2,1)} copy(bf16[512,256]{1,0:T(8,128)(2,1)} %get-tuple-element.12) | data formatting | bytes 524288
  127.3 0.0 copy-done
  127.3 0.7 copy.20
  128.0 0.0 copy-done.1
  128.0 0.7 copy.21
Async XLA Ops:
  122.1 5.3 %copy-start = (bf16[512,256]{1,0:T(8,128)(2,1)S(1)}, bf16[512,256]{1,0:T(8,128)(2,1)}, u32[]{:S(2)}) copy-start(bf16[512,256]{1,0:T(8,128)(2,1)} %get-tuple-element.13) | copy-start | bytes 786436
  122.1 6.0 %copy-start.1 = (f32[256,128]{1,0:T(8,128)S(1)}, f32[256,128]{1,0:T(8,128)}, u32[]{:S(2)}) copy-start(f32[256,128]{1,0:T(8,128)} %get-tuple-element.14) | copy-start | bytes 393220

commit v2 on v1

--- a/solution.py
+++ b/solution.py
@@ -12,6 +12,7 @@
 T = 512
 CT = 1024
 SUB = 256
+NX = 4
 REACH = 4
 DOCS = 24
 TOOLS = 16
@@ -48,9 +49,10 @@
     seg, tool, q_in, k_in, v_in, w_in, gm_in,
     out, dq_out, dk_out, dv_out, gw_out,
     qs, kv, fk, qt, m_s, l_s, ot, otb, ob, gmf, da, dos, dob, dotr, dqt, wsl, atf, lo,
-    d0, sa, sb, s4, ra, rb, rf, rf4, fin, pg, gown, gws, gwr, gsum, gwi,
-    swap_s, swap_r, kv_s, kv_r, zg_s, zg_r, za_s, za_r, w1_s, w1_r, w2_s, w2_r,
-    w3_s, w3_r, at_s, at_r, do_s, do_r, ch_s, ch_r, fn_s, fn_r, gx_s, gx_r, gw_s, gw_r,
+    acc, snd, r1, r2, r3, fin, pg, gown, gws, gwr, ysend, yin, xown, xsend, xin,
+    swap_s, swap_r, kv_s, kv_r, zg_s, zg_r, za_s, za_r, w1_s, w1_r, wx_s, wx_r, wy_s, wy_r,
+    w3_s, w3_r, at_s, at_r, do_s, do_r, c1_s, c1_r, c2_s, c2_r, c3_s, c3_r,
+    fn_s, fn_r, gx_s, gx_r, gy_s, gy_r, gt_s, gt_r,
 ):
     me = lax.axis_index("ctx")
     z = lax.axis_index("head")
@@ -59,11 +61,15 @@
     o = 1 - c
     sib = me + 1 - 2 * c
 
+    ny = nc // NX
+    y = m // NX
+    x = lax.rem(m, NX)
+
     def chip(by):
         return lax.rem(m + by + nc, nc)
 
-    def at_chip(by):
-        return 2 * chip(by) + c
+    def mate(dy, dx):
+        return 2 * (lax.rem(y + dy + ny, ny) * NX + lax.rem(x + dx + NX, NX)) + c
 
     def zed(by):
         return lax.rem(z + by + nz, nz)
@@ -86,15 +92,16 @@
     barrier = pltpu.get_barrier_semaphore()
     pl.semaphore_signal(barrier, inc=1, device_id=(sib, z), device_id_type=MESH)
 
-    @pl.loop(1, nc)
-    def _(by):
-        pl.semaphore_signal(barrier, inc=1, device_id=(at_chip(by), z), device_id_type=MESH)
+    for by in range(1, NX):
+        pl.semaphore_signal(barrier, inc=1, device_id=(mate(0, by), z), device_id_type=MESH)
+    for by in range(1, ny):
+        pl.semaphore_signal(barrier, inc=1, device_id=(mate(by, 0), z), device_id_type=MESH)
 
     @pl.loop(1, nz)
     def _(by):
         pl.semaphore_signal(barrier, inc=1, device_id=(me, zed(by)), device_id_type=MESH)
 
-    pl.semaphore_wait(barrier, 1 + (nc - 1) + (nz - 1))
+    pl.semaphore_wait(barrier, 1 + (NX - 1) + (ny - 1) + (nz - 1))
 
     for t, (src, dst) in enumerate(((q_in, qs.at[c]), (k_in, kv.at[0, c, 0]), (v_in, kv.at[0, c, 1]))):
         start(remote(src.at[:, cols(o, HD)], dst, swap_s.at[t], swap_r.at[t], sib, z))
@@ -140,14 +147,51 @@
     kv[0, c, 0] = k_in[:, cols(c, HD)]
     kv[0, c, 1] = v_in[:, cols(c, HD)]
 
+    for t, dst in enumerate((qs.at[o], kv.at[0, o, 0], kv.at[0, o, 1])):
+        remote(dst, dst, swap_s.at[t], swap_r.at[t], sib, z).wait_recv()
+
+    inner = (x == 1) | (x == 2)
+
+    def kv_copy(slot, h):
+        if slot == 1:
+            src, to = jnp.where(x < NX - 1, 0, REACH), mate(0, 1)
+        elif slot == 3:
+            src, to = jnp.where(x > 0, REACH, 0), mate(0, -1)
+        else:
+            src, to = 0, mate(1, 0)
+        return remote(kv.at[src, h], kv.at[slot, h], kv_s.at[slot, h], kv_r.at[slot, h], to, z)
+
+    def kv_on(side, h):
+        src, to = ((1, mate(0, 1)), (3, mate(0, -1)))[side]
+        return remote(kv.at[src, h], kv.at[2, h], kv_s.at[5 + side, h], kv_r.at[2, h], to, z)
+
+    def kv_recv(slot, h):
+        remote(kv.at[slot, h], kv.at[slot, h], kv_s.at[slot, h], kv_r.at[slot, h], me, z).wait_recv()
+
+    def kv_forward(slot, h):
+        kv_recv(slot, h)
+        if slot == REACH:
+            pl.when(x == NX - 1)(kv_copy(1, h).start)
+            pl.when(x > 0)(kv_copy(3, h).start)
+        else:
+            pl.when(inner)(kv_on(slot // 2, h).start)
+
+    for h in range(2):
+        kv_copy(REACH, h).start()
+        pl.when(x < NX - 1)(kv_copy(1, h).start)
+        pl.when(x == 0)(kv_copy(3, h).start)
+
+    def ids(ref, index):
+        rows = ref[pl.ds(pl.multiple_of(index * 8, 8), 8), :]
+        return jnp.concatenate([rows[r:r + 1, :] for r in range(8)], axis=1)
+
     row = lax.broadcasted_iota(jnp.int32, (HD, CT), 0)
     pos = lax.broadcasted_iota(jnp.int32, (HD, CT), 1)
     block64 = lax.shift_right_logical(pos, 6)
     is_doc = row < DOCS
     is_tool = (row >= DOCS) & (row < LSE_ROW)
     for d in range(REACH + 1):
-        seg_row = seg[pl.ds(chip(-d), 1), :]
-        tool_row = tool[pl.ds(chip(-d), 1), :]
+        seg_row, tool_row = ids(seg, chip(-d)), ids(tool, chip(-d))
         if d == 0:
             bad_tool = (block64 > row - DOCS) | ((tool_row != 0) & (block64 != row - DOCS))
         else:
@@ -155,31 +199,10 @@
         bad = (is_doc & (seg_row != row)) | (is_tool & bad_tool)
         feat = jnp.where(bad, -MASK, jnp.where((row >= LSE_ROW) & (row < LSE_ROW + 3), -1.0, 0.0))
         fk[d] = feat.T.astype(BF16)
-    seg_row = seg[pl.ds(m, 1), :]
+    seg_row = ids(seg, m)
     hot = (is_doc & (seg_row == row)) | (is_tool & (block64 == row - DOCS))
     qfeat = jnp.where(hot, 1.0, 0.0)
     qt[HD:, :] = qfeat.astype(BF16)
-
-    for t, dst in enumerate((qs.at[o], kv.at[0, o, 0], kv.at[0, o, 1])):
-        remote(dst, dst, swap_s.at[t], swap_r.at[t], sib, z).wait_recv()
-
-    kv_moves = {
-        (1, 0): (0, 1), (3, 1): (0, 3), (4, 0): (0, 4), (4, 1): (0, 4),
-        (2, 0): (1, 1), (3, 0): (2, 1), (2, 1): (3, -1), (1, 1): (2, -1),
-    }
-    kv_key = {key: index for index, key in enumerate(kv_moves)}
-
-    def kv_send(key):
-        source, by = kv_moves[key]
-        k = kv_key[key]
-        start(remote(kv.at[source, key[1]], kv.at[key], kv_s.at[k], kv_r.at[k], at_chip(by), z))
-
-    def kv_recv(key):
-        k = kv_key[key]
-        remote(kv.at[key], kv.at[key], kv_s.at[k], kv_r.at[k], me, z).wait_recv()
-
-    for key in ((1, 0), (3, 1), (4, 0), (4, 1)):
-        kv_send(key)
 
     qt[:HD, :] = jnp.concatenate([qs[0].astype(F32).T, qs[1].astype(F32).T], axis=1).astype(BF16)
     m_s[...] = jnp.full(m_s.shape, -1e30, F32)
@@ -232,47 +255,47 @@
         ring_recv(gmf, zg_s, zg_r, step, half)
         ring_send(gmf, zg_s, zg_r, step + 1, half)
 
-    def kv_step(key, then=None):
-        kv_recv(key)
-        if then is not None:
-            kv_send(then)
-
     forward((0, 0))
     forward((0, 1))
-    kv_step((1, 0), (2, 0))
     gm_step(0)
+    kv_forward(4, 0)
+    forward((4, 0))
+    grad_block(z)
+    gm_step(1)
+    kv_forward(4, 1)
+    kv_forward(1, 0)
+    kv_forward(3, 0)
+    forward((4, 1))
     forward((1, 0))
-    kv_step((3, 1), (2, 1))
-    grad_block(z)
-    forward((3, 1))
-    kv_step((2, 0), (3, 0))
-    gm_step(1)
-    forward((2, 0))
-    kv_step((2, 1), (1, 1))
-    forward((2, 1))
-    kv_recv((4, 0))
-    forward((4, 0))
-    grad_block(zed(1))
-    grad_block(zed(-1))
-    gm_step(2)
-    kv_recv((3, 0))
-    forward((3, 0))
-    kv_recv((4, 1))
-    forward((4, 1))
 
     @pl.loop(1, nz)
     def _(by):
         src = wsl.at[zed(-by), rows16, wide]
         remote(src, src, w1_s.at[by], w1_r.at[by], me, z).wait_recv()
 
+    for by in range(1, NX):
+        src = wsl.at[:, rows16, wide]
+        start(remote(src, src, wx_s.at[by], wx_r.at[by], mate(0, by), z))
+    gm_step(2)
+    kv_forward(1, 1)
+    kv_forward(3, 1)
+    forward((1, 1))
+    forward((3, 0))
+    grad_block(zed(1))
+    grad_block(zed(-1))
     gm_step(3)
-    kv_recv((1, 1))
-    forward((1, 1))
-
-    @pl.loop(1, nc)
-    def _(by):
-        src = wsl.at[:, rows16, wide]
-        remote(src, src, w2_s.at[by], w2_r.at[by], at_chip(by), z).start()
+    kv_recv(2, 0)
+    forward((3, 1))
+    forward((2, 0))
+    for by in range(1, NX):
+        src = wsl.at[:, pl.ds(pl.multiple_of((y * NX + lax.rem(x - by + NX, NX)) * 16, 16), 16), wide]
+        remote(src, src, wx_s.at[by], wx_r.at[by], me, z).wait_recv()
+    for by in range(1, ny):
+        src = wsl.at[:, pl.ds(pl.multiple_of(y * NX * 16, 16), NX * 16), wide]
+        start(remote(src, src, wy_s.at[by], wy_r.at[by], mate(by, 0), z))
+    gm_step(4)
+    kv_recv(2, 1)
+    forward((2, 1))
 
     inv = 1.0 / l_s[...]
     lse = m_s[...] + jnp.log2(l_s[...]) * (1.0 / LOG2)
@@ -291,25 +314,26 @@
     dst = atf.at[z, :, :, cols(o, HD)]
     remote(dst, dst, at_s, at_r, sib, z).wait_recv()
 
-    def weight_block(block):
+    order = (0, 1, -1, 2, -2, 3, -3, 4)
+    per = nc // nz
+
+    def weight_block(index):
+        block = zed(order[index])
         part = dot_tn(atf[z, 0], gmf[block, 0]) + dot_tn(atf[z, 1], gmf[block, 1])
         pg[...] = part
-        per = nc // nz
         for e in range(per):
             gown[block * per + e] = pg[:, pl.ds(pl.multiple_of(e * SUB + c * HD, HD), HD)]
             gws[block * per + e] = pg[:, pl.ds(pl.multiple_of(e * SUB + o * HD, HD), HD)].astype(BF16)
 
     grad_block(zed(2))
     grad_block(zed(-2))
-    for by in (0, 1, -1, 2, -2):
-        weight_block(zed(by))
-    gm_step(4)
     gm_step(5)
     for half in range(2):
         ring_send(atf, za_s, za_r, 1, half)
-    for by in (3, -3):
-        grad_block(zed(by))
-        weight_block(zed(by))
+    for index in range(5):
+        weight_block(index)
+    grad_block(zed(3))
+    grad_block(zed(-3))
     gm_step(6)
     gm_step(7)
     grad_block(zed(4))
@@ -317,8 +341,8 @@
     dos[...] = da[:, cols(o, HD)].astype(BF16)
     start(remote(dos, dob.at[c], do_s, do_r, sib, z))
     dob[c] = da[:, mine].astype(BF16)
-
-    weight_block(zed(4))
+    for index in range(5, 8):
+        weight_block(index)
     start(remote(gws, gwr, gx_s, gx_r, sib, z))
 
     remote(dob.at[o], dob.at[o], do_s, do_r, sib, z).wait_recv()
@@ -351,74 +375,97 @@
             finish(rows, dot(ds, q_rows) * SCALE, dot(p.astype(BF16), do_rows))
             dqt[:, q0:q0 + qn] = dqt[:, q0:q0 + qn] + dot_tn(k_tile, ds)
 
-    def keep(buf, *slot):
+    def grads(slot, h):
         def finish(rows, dk, dv):
-            buf[(*slot, 0, rows)] = dk.astype(buf.dtype)
-            buf[(*slot, 1, rows)] = dv.astype(buf.dtype)
-        return finish
-
-    def add_keep(buf, other, *slot):
-        def finish(rows, dk, dv):
-            buf[(*slot, 0, rows)] = (dk + other[(*slot, 0, rows)].astype(F32)).astype(BF16)
-            buf[(*slot, 1, rows)] = (dv + other[(*slot, 1, rows)].astype(F32)).astype(BF16)
-        return finish
+            acc[slot, h, 0, rows] = dk
+            acc[slot, h, 1, rows] = dv
+
+        backward((slot, h), finish)
+
+    def gate(cond):
+        return jnp.where(cond, 1.0, 0.0).astype(F32)
+
+    side = jnp.where(x < 2, 0, 1)
+
+    def back1(h):
+        to = jnp.where(x < 2, mate(0, 1), mate(0, -1))
+        return remote(snd.at[2, h], r1.at[side, h], c1_s.at[h], c1_r.at[side, h], to, z)
+
+    def back1_add(h):
+        for half in range(2):
+            slot = 3 - 2 * half
+
+            @pl.when(inner)
+            def _():
+                remote(r1.at[half, h], r1.at[half, h], c1_s.at[h], c1_r.at[half, h], me, z).wait_recv()
+                snd[slot, h] = (acc[slot, h] + r1[half, h].astype(F32)).astype(BF16)
+
+            @pl.when(jnp.logical_not(inner))
+            def _():
+                snd[slot, h] = acc[slot, h].astype(BF16)
+
+        start(remote(snd.at[3, h], r2.at[0, h], c2_s.at[0, h], c2_r.at[0, h], mate(0, 1), z))
+        start(remote(snd.at[1, h], r2.at[1, h], c2_s.at[1, h], c2_r.at[1, h], mate(0, -1), z))
+
+    def back2_add(h):
+        for half in range(2):
+            remote(r2.at[half, h], r2.at[half, h], c2_s.at[half, h], c2_r.at[half, h], me, z).wait_recv()
+        a, b = r2[0, h].astype(F32), r2[1, h].astype(F32)
+        snd[REACH, h] = (acc[REACH, h] + a * gate(x > 0) + b * gate(x == NX - 1)).astype(BF16)
+        start(remote(snd.at[REACH, h], r3.at[h], c3_s.at[h], c3_r.at[h], mate(-1, 0), z))
+        acc[0, h] = acc[0, h] + a * gate(x == 0) + b * gate(x < NX - 1)
 
     def att_step(k):
         step, half = k // 2 + 1, k % 2
         ring_recv(atf, za_s, za_r, step, half)
         ring_send(atf, za_s, za_r, step + 1, half)
 
-    def stage(s):
-        a, b = (s, 0), (REACH - s, 1)
-        if s == 1:
-            backward(a, keep(sa, 0))
-        else:
-            remote(ra.at[s - 1], ra.at[s - 1], ch_s.at[s - 2], ch_r.at[s - 2], me, z).wait_recv()
-            backward(a, add_keep(sa, ra, s - 1))
-        if s < REACH - 1:
-            start(remote(sa.at[s - 1], ra.at[s], ch_s.at[s - 1], ch_r.at[s - 1], at_chip(1), z))
-        else:
-            start(remote(sa.at[s - 1], rf.at[0], ch_s.at[s - 1], ch_r.at[s - 1], at_chip(-3), z))
-        if s == 1:
-            backward(b, keep(sb, 0))
-        else:
-            remote(rb.at[s - 1], rb.at[s - 1], ch_s.at[s + 1], ch_r.at[s + 1], me, z).wait_recv()
-            backward(b, add_keep(sb, rb, s - 1))
-        if s < REACH - 1:
-            start(remote(sb.at[s - 1], rb.at[s], ch_s.at[s + 2], ch_r.at[s + 2], at_chip(-1), z))
-        else:
-            start(remote(sb.at[s - 1], rf.at[1], ch_s.at[s + 2], ch_r.at[s + 2], at_chip(-1), z))
-
-    stage(1)
+    for h in range(2):
+        grads(2, h)
+        snd[2, h] = acc[2, h].astype(BF16)
+        start(back1(h))
     att_step(0)
+    grads(1, 0)
+    grads(3, 0)
+    att_step(1)
+    back1_add(0)
+    grads(1, 1)
+    att_step(2)
+    grads(3, 1)
+    back1_add(1)
+    att_step(3)
 
     remote(gwr, gwr, gx_s, gx_r, sib, z).wait_recv()
 
-    @pl.loop(1, nc)
-    def _(by):
-        to = lax.rem(m + by, nc)
-        gsum[to] = (gown[to] + gwr[to].astype(F32)).astype(BF16)
-        remote(gsum.at[to], gwi.at[by], gw_s.at[by], gw_r.at[by], at_chip(by), z).start()
-
-    att_step(1)
-    for h in range(2):
-        backward((REACH, h), keep(s4, h))
-    start(remote(s4, rf4, ch_s.at[6], ch_r.at[6], at_chip(-4), z))
-    att_step(2)
-    stage(2)
-    att_step(3)
-    for h in range(2):
-        backward((0, h), keep(d0, h))
-
-    @pl.loop(1, nc)
-    def _(by):
-        src = wsl.at[:, pl.ds(pl.multiple_of(chip(-by) * 16, 16), 16), wide]
-        remote(src, src, w2_s.at[by], w2_r.at[by], me, z).wait_recv()
-
+    def row_of(by):
+        return pl.ds(lax.rem(y + by, ny) * NX, NX)
+
+    for by in range(1, ny):
+        ysend[by] = (gown[row_of(by)] + gwr[row_of(by)].astype(F32)).astype(BF16)
+        start(remote(ysend.at[by], yin.at[by], gy_s.at[by], gy_r.at[by], mate(by, 0), z))
+
+    for by in range(1, ny):
+        src = wsl.at[:, pl.ds(pl.multiple_of(lax.rem(y - by + ny, ny) * NX * 16, 16), NX * 16), wide]
+        remote(src, src, wy_s.at[by], wy_r.at[by], me, z).wait_recv()
     start(remote(wsl.at[:, :, wide], wsl.at[:, :, wide], w3_s, w3_r, sib, z))
+
+    grads(4, 0)
     att_step(4)
+    grads(4, 1)
+    grads(0, 0)
     att_step(5)
-    stage(3)
+    grads(0, 1)
+    back2_add(0)
+
+    xown[...] = gown[row_of(0)] + gwr[row_of(0)].astype(F32)
+    for by in range(1, ny):
+        remote(yin.at[by], yin.at[by], gy_s.at[by], gy_r.at[by], me, z).wait_recv()
+        xown[...] = xown[...] + yin[by].astype(F32)
+    for by in range(1, NX):
+        xsend[by] = xown[lax.rem(x + by, NX)].astype(BF16)
+        start(remote(xsend.at[by], xin.at[by], gt_s.at[by], gt_r.at[by], mate(0, by), z))
+
+    back2_add(1)
 
     fin[0, 0] = (dqt[:, :T] * SCALE).T.astype(BF16)
     fin[0, 1] = (dqt[:, T:] * SCALE).T.astype(BF16)
@@ -439,10 +486,10 @@
     for by in (1, -1, 2, -2, 3, -3):
         out_block(zed(by))
 
-    total = gown[m] + gwr[m].astype(F32)
-    for by in range(1, nc):
-        remote(gwi.at[by], gwi.at[by], gw_s.at[by], gw_r.at[by], me, z).wait_recv()
-        total = total + gwi[by].astype(F32)
+    total = xown[x]
+    for by in range(1, NX):
+        remote(xin.at[by], xin.at[by], gt_s.at[by], gt_r.at[by], me, z).wait_recv()
+        total = total + xin[by].astype(F32)
     gw_out[...] = total
 
     att_step(6)
@@ -450,11 +497,10 @@
     out_block(zed(4))
     out[...] = lo[...].astype(BF16)
 
-    remote(rf4, rf4, ch_s.at[6], ch_r.at[6], me, z).wait_recv()
     for h in range(2):
-        remote(rf.at[h], rf.at[h], ch_s.at[2 + 3 * h], ch_r.at[2 + 3 * h], me, z).wait_recv()
+        remote(r3.at[h], r3.at[h], c3_s.at[h], c3_r.at[h], me, z).wait_recv()
         for t in range(2):
-            fin[1 + t, h] = (d0[h, t] + rf[h, t].astype(F32) + rf4[h, t].astype(F32)).astype(BF16)
+            fin[1 + t, h] = (acc[0, h, t] + r3[h, t].astype(F32)).astype(BF16)
     for t in (1, 2):
         start(remote(fin.at[t, o], outs[t].at[:, mine], fn_s.at[t], fn_r.at[t], sib, z))
         outs[t][:, mine] = fin[t, c]
@@ -470,11 +516,16 @@
         src = wsl.at[z, rows16, wide]
         remote(src, src, w1_s.at[by], w1_r.at[by], me, zed(by)).wait_send()
 
-    @pl.loop(1, nc)
-    def _(by):
-        src = wsl.at[:, rows16, wide]
-        remote(src, src, w2_s.at[by], w2_r.at[by], at_chip(by), z).wait_send()
-        remote(gwi.at[by], gwi.at[by], gw_s.at[by], gw_r.at[by], at_chip(by), z).wait_send()
+    for h in range(2):
+        for slot in (1, 3, REACH):
+            kv_copy(slot, h).wait_send()
+        for half in range(2):
+            pl.when(inner)(kv_on(half, h).wait_send)
+
+
+def copy_kernel(*refs):
+    for src, dst in zip(refs[:5], refs[5:]):
+        dst[...] = src[...]
 
 
 def body(nc, nz, queries, key_in, values, segment, tool_ids, out_weight, grad_mixed):
@@ -501,25 +552,27 @@
         vm((nz, 2 * HD, T), BF16),
         vm((nz, 2, SUB, 2 * HD), BF16),
         vm((T, T), F32),
-        vm((2, *grads), F32),
-        vm((3, *grads), BF16), vm((3, *grads), BF16),
-        vm((2, *grads), BF16),
-        vm((3, *grads), BF16), vm((3, *grads), BF16),
-        vm((2, *grads), BF16), vm((2, *grads), BF16),
+        vm((REACH + 1, 2, *grads), F32),
+        vm((REACH + 1, 2, *grads), BF16),
+        vm((2, 2, *grads), BF16), vm((2, 2, *grads), BF16), vm((2, *grads), BF16),
         vm((3, 2, T, HD), BF16),
         vm((2 * HD, T), F32),
         vm((nc, 2 * HD, HD), F32),
         vm((nc, 2 * HD, HD), BF16), vm((nc, 2 * HD, HD), BF16),
-        vm((nc, 2 * HD, HD), BF16), vm((nc, 2 * HD, HD), BF16),
+        vm((nc // NX, NX, 2 * HD, HD), BF16), vm((nc // NX, NX, 2 * HD, HD), BF16),
+        vm((NX, 2 * HD, HD), F32),
+        vm((NX, 2 * HD, HD), BF16), vm((NX, 2 * HD, HD), BF16),
         dma((3,)), dma((3,)),
-        dma((8,)), dma((8,)),
+        dma((7, 2)), dma((REACH + 1, 2)),
         dma((16,)), dma((16,)), dma((16,)), dma((16,)),
-        dma((nz,)), dma((nz,)), dma((nc,)), dma((nc,)), one, one,
+        dma((nz,)), dma((nz,)),
+        dma((NX,)), dma((NX,)), dma((nc // NX,)), dma((nc // NX,)), one, one,
         one, one, one, one,
-        dma((7,)), dma((7,)), dma((3,)), dma((3,)),
-        one, one, dma((nc,)), dma((nc,)),
+        dma((2,)), dma((2, 2)), dma((2, 2)), dma((2, 2)), dma((2,)), dma((2,)),
+        dma((3,)), dma((3,)), one, one,
+        dma((nc // NX,)), dma((nc // NX,)), dma((NX,)), dma((NX,)),
     ]
-    return pl.pallas_call(
+    results = pl.pallas_call(
         functools.partial(kernel, nc, nz),
         out_shape=(
             jax.ShapeDtypeStruct((T, width // nz), BF16),
@@ -538,9 +591,15 @@
             flops=20_000_000_000, bytes_accessed=8_000_000, transcendentals=10_000_000
         ),
     )(
-        segment.reshape(nc, CT), tool_ids.reshape(nc, CT),
+        segment.reshape(-1, HD), tool_ids.reshape(-1, HD),
         queries, key_in, values, out_weight, grad_mixed.reshape(2, SUB, width // nz),
     )
+    return pl.pallas_call(
+        copy_kernel,
+        out_shape=tuple(jax.ShapeDtypeStruct(r.shape, r.dtype) for r in results),
+        in_specs=[pl.BlockSpec(memory_space=pltpu.VMEM)] * 5,
+        out_specs=[pl.BlockSpec(memory_space=pltpu.VMEM)] * 5,
+    )(*results)
 
 
 def solution(mesh):

time: 129 us -> 105 us (0.81)
  the two profiles are of different devices: /device:TPU:1 before, /device:TPU:19 now
where the time goes in v2:
time: 105 us
  Pallas kernels  104 us (99%)
    pallas_call x1, Pallas kernels, body(): pl.pallas_call(functools.partial(kernel, nc, nz), out_shape=(jax.ShapeDty...  102 us
    pallas_call x1, Pallas kernels, body(): pl.pallas_call(copy_kernel, out_shape=tuple((jax.ShapeDtypeStruct(r.shape...  2.41 us

profile of v2, /device:TPU:19, one launch (start us, length us, event | category | flops | bytes accessed | tf_op | source)
XLA Modules:
  0.0 105.1 jit_solution(3971829556673961690)
XLA Ops:
  0.6 102.0 %shard_map.110 = (bf16[512,512]{1,0:T(8,128)(2,1)}, bf16[512,256]{1,0:T(8,128)(2,1)}, bf16[512,256]{1,0:T(8,128)(2,1)}, bf16[512,256]{1,0:T(8,128)(2,1)}, f32[256,128]{1,0:T(8,128)}) custom-call(s32[128,128]{1,0:T(8,128)} %bitcast.4, s32[128,128]{1,0:T(8,128)} %bitcast.5, bf16[512,256]{1,0:T(8,128)(2,1)} %q_in.1, bf16[512,256]{1,0:T(8,128)(2,1)} %k_in.1, ...), custom_call_target="tpu_custom_call" | custom-call | flops 20000000000 | bytes 8000000 | tf_op jit(solution)/shard_map/pallas_call | solution.py:575
  102.7 2.4 %shard_map.111 = (bf16[512,512]{1,0:T(8,128)(2,1)}, bf16[512,256]{1,0:T(8,128)(2,1)}, bf16[512,256]{1,0:T(8,128)(2,1)}, bf16[512,256]{1,0:T(8,128)(2,1)}, f32[256,128]{1,0:T(8,128)}) custom-call(bf16[512,512]{1,0:T(8,128)(2,1)} %get-tuple-element.10.refs_0_, bf16[512,256]{1,0:T(8,128)(2,1)} %get-tuple-element.11.refs_1_, ...), custom_call_target="tpu_custom_call" | custom-call | tf_op jit(solution)/shard_map/pallas_call | solution.py:597

commit v3 on v2

v3 whole, which is shorter than its diff:
```python
import functools
import math

import jax
import jax.numpy as jnp
from jax import lax
from jax.experimental import pallas as pl
from jax.experimental.pallas import tpu as pltpu
from jax.sharding import PartitionSpec as P

HD = 128
T = 512
CT = 1024
SUB = 256
NX = 4
REACH = 4
DOCS = 24
TOOLS = 16
LSE_ROW = DOCS + TOOLS
MASK = 131072.0
SCALE = 1.0 / math.sqrt(HD)
LOG2 = SCALE * math.log2(math.e)
MESH = pl.DeviceIdType.MESH
F32 = jnp.float32
BF16 = jnp.bfloat16


def dot(a, b):
    return jnp.dot(a, b, preferred_element_type=F32)


def dot_tn(a, b):
    return lax.dot_general(a, b, (((0,), (0,)), ((), ())), preferred_element_type=F32)


def dot_nt(a, b):
    return lax.dot_general(a, b, (((1,), (1,)), ((), ())), preferred_element_type=F32)


def thirds(x):
    high = x.astype(BF16)
    rest = x - high.astype(F32)
    mid = rest.astype(BF16)
    return high.astype(F32), mid.astype(F32), (rest - mid.astype(F32))


def kernel(
    nc, nz,
    seg, tool, q_in, k_in, v_in, w_hbm, gm_in,
    out, dq_out, dk_out, dv_out, gw_out,
    qw, kv, fk, qt, qtmp, m_s, l_s, ot, otb, ob, gmf, da, dos, dow, dot_t, dtmp, dqt, wsl, atf, lo, st,
    w_in, acc, fin, pg, gown, gws, gwr, ysend, yin, xown, xsend, xin,
    swap_s, swap_r, kv_s, kv_r, zg_s, zg_r, za_s, za_r, w1_s, w1_r, wx_s, wx_r, wy_s, wy_r,
    w3_s, w3_r, at_s, at_r, do_s, do_r, q_s, q_r, d_s, d_r, t_s, t_r,
    fn_s, fn_r, gx_s, gx_r, gy_s, gy_r, gt_s, gt_r, local_s,
):
    me = lax.axis_index("ctx")
    z = lax.axis_index("head")
    m = me // 2
    c = lax.rem(me, 2)
    o = 1 - c
    sib = me + 1 - 2 * c

    ny = nc // NX
    y = m // NX
    x = lax.rem(m, NX)

    def chip(by):
        return lax.rem(m + by + nc, nc)

    def mate(dy, dx):
        return 2 * (lax.rem(y + dy + ny, ny) * NX + lax.rem(x + dx + NX, NX)) + c

    def zed(by):
        return lax.rem(z + by + nz, nz)

    def remote(src, dst, ss, rs, ctx, head):
        return pltpu.make_async_remote_copy(
            src_ref=src, dst_ref=dst, send_sem=ss, recv_sem=rs,
            device_id=(ctx, head), device_id_type=MESH,
        )

    def cols(index, width):
        return pl.ds(pl.multiple_of(index * width, width), width)

    sent = []

    def start(copy):
        copy.start()
        sent.append(copy)

    local = [
        pltpu.make_async_copy(src, dst, local_s.at[index])
        for index, (src, dst) in enumerate((
            (w_hbm, w_in),
            (gm_in, gmf.at[z]),
            (q_in.at[:, :, cols(c, HD)], qw.at[0, :, c]),
            (k_in.at[:, cols(c, HD)], kv.at[0, c, 0]),
            (v_in.at[:, cols(c, HD)], kv.at[0, c, 1]),
        ))
    ]
    for copy in local:
        copy.start()

    barrier = pltpu.get_barrier_semaphore()
    pl.semaphore_signal(barrier, inc=1, device_id=(sib, z), device_id_type=MESH)

    for by in range(1, NX):
        pl.semaphore_signal(barrier, inc=1, device_id=(mate(0, by), z), device_id_type=MESH)
    for by in range(1, ny):
        pl.semaphore_signal(barrier, inc=1, device_id=(mate(by, 0), z), device_id_type=MESH)

    @pl.loop(1, nz)
    def _(by):
        pl.semaphore_signal(barrier, inc=1, device_id=(me, zed(by)), device_id_type=MESH)

    pl.semaphore_wait(barrier, 1 + (NX - 1) + (ny - 1) + (nz - 1))

    swaps = (
        (q_in.at[:, :, cols(o, HD)], qw.at[0, :, c], qw.at[0, :, o]),
        (k_in.at[:, cols(o, HD)], kv.at[0, c, 0], kv.at[0, o, 0]),
        (v_in.at[:, cols(o, HD)], kv.at[0, c, 1], kv.at[0, o, 1]),
    )
    for t, (src, dst, _) in enumerate(swaps):
        start(remote(src, dst, swap_s.at[t], swap_r.at[t], sib, z))

    full = nz // 2 - 1

    def ring_has(step, part, parts, right):
        return step <= full or (step == full + 1 and (part * 2 < parts) == right)

    def ring_send(buf, ss, rs, step, part, parts, src=None):
        for side, right in enumerate((True, False)):
            if ring_has(step, part, parts, right):
                block = zed(1 - step) if right else zed(step - 1)
                to = zed(1) if right else zed(-1)
                k = (side * (full + 1) + step - 1) * parts + part
                dst = buf.at[block, part]
                start(remote(dst if src is None else src, dst, ss.at[k], rs.at[k], me, to))

    def ring_recv(buf, ss, rs, step, part, parts):
        for side, right in enumerate((True, False)):
            if ring_has(step, part, parts, right):
                block = zed(-step) if right else zed(step)
                k = (side * (full + 1) + step - 1) * parts + part
                dst = buf.at[block, part]
                remote(dst, dst, ss.at[k], rs.at[k], me, z).wait_recv()

    def gm_send(j):
        for part in (2 * j, 2 * j + 1):
            ring_send(gmf, zg_s, zg_r, 1, part, 4, gm_in.at[part])

    def gm_step(j, step):
        for part in (2 * j, 2 * j + 1):
            ring_recv(gmf, zg_s, zg_r, step, part, 4)
            ring_send(gmf, zg_s, zg_r, step + 1, part, 4)

    gm_send(0)

    for copy in local:
        copy.wait()

    rows16 = pl.ds(pl.multiple_of(m * 16, 16), 16)
    wide = cols(c, SUB)

    @pl.loop(1, nz)
    def _(by):
        to = zed(by)
        src = w_in.at[rows16, pl.ds(pl.multiple_of(to * T + c * SUB, SUB), SUB)]
        remote(src, wsl.at[z, rows16, wide], w1_s.at[by], w1_r.at[by], me, to).start()

    wsl[z, rows16, wide] = w_in[rows16, pl.ds(pl.multiple_of(z * T + c * SUB, SUB), SUB)]

    for t, (_, _, dst) in enumerate(swaps):
        remote(dst, dst, swap_s.at[t], swap_r.at[t], sib, z).wait_recv()

    inner = (x == 1) | (x == 2)

    class Tree:
        def __init__(self, buf, ss, rs, sign):
            self.refs = buf, ss, rs
            self.sign = sign
            self.at = x if sign > 0 else NX - 1 - x

        def copy(self, slot, i):
            buf, ss, rs = self.refs
            if slot == 1:
                src, to = jnp.where(self.at < NX - 1, 0, REACH), mate(0, self.sign)
            elif slot == 3:
                src, to = jnp.where(self.at > 0, REACH, 0), mate(0, -self.sign)
            else:
                src, to = 0, mate(self.sign, 0)
            return remote(buf.at[src, i], buf.at[slot, i], ss.at[slot, i], rs.at[slot, i], to, z)

        def on(self, slot, i):
            buf, ss, rs = self.refs
            to = mate(0, self.sign if slot == 1 else -self.sign)
            return remote(buf.at[slot, i], buf.at[2, i], ss.at[5 + slot // 2, i], rs.at[2, i], to, z)

        def first(self, i):
            pl.when(self.at < NX - 1)(self.copy(1, i).start)
            pl.when(self.at == 0)(self.copy(3, i).start)
            self.copy(REACH, i).start()

        def take(self, slot, i):
            buf, ss, rs = self.refs
            remote(buf.at[slot, i], buf.at[slot, i], ss.at[slot, i], rs.at[slot, i], me, z).wait_recv()
            if slot == REACH:
                pl.when(self.at == NX - 1)(self.copy(1, i).start)
                pl.when(self.at > 0)(self.copy(3, i).start)
            elif slot != 2:
                pl.when(inner)(self.on(slot, i).start)

        def drain(self):
            for i in range(2):
                for slot in (1, 3, REACH):
                    self.copy(slot, i).wait_send()
                for slot in (1, 3):
                    pl.when(inner)(self.on(slot, i).wait_send)

    kvs = Tree(kv, kv_s, kv_r, 1)
    qts = Tree(qw, q_s, q_r, -1)
    dts = Tree(dow, d_s, d_r, -1)
    sts = Tree(st, t_s, t_r, -1)
    for i in range(2):
        kvs.first(i)

    def ids(ref, index, order=(0, 1, 2, 3, 4, 5, 6, 7)):
        rows = ref[pl.ds(pl.multiple_of(index * 8, 8), 8), :]
        return jnp.concatenate([rows[r:r + 1, :] for r in order], axis=1)

    row = lax.broadcasted_iota(jnp.int32, (HD, CT), 0)
    pos = lax.broadcasted_iota(jnp.int32, (HD, CT), 1)
    block64 = lax.shift_right_logical(pos, 6)
    is_doc = row < DOCS
    is_tool = (row >= DOCS) & (row < LSE_ROW)
    for d in range(REACH + 2):
        back = -d if d <= REACH else 0
        seg_row, tool_row = ids(seg, chip(back)), ids(tool, chip(back))
        if d == 0:
            bad_tool = (block64 > row - DOCS) | ((tool_row != 0) & (block64 != row - DOCS))
        else:
            bad_tool = jnp.broadcast_to(tool_row != 0, row.shape)
        bad = (is_doc & (seg_row != row)) | (is_tool & bad_tool)
        feat = jnp.where(bad, -MASK, jnp.where((row >= LSE_ROW) & (row < LSE_ROW + 3), -1.0, 0.0))
        fk[d] = feat.T.astype(BF16)

    half_row = lax.broadcasted_iota(jnp.int32, (HD, T), 0)
    half_pos = lax.broadcasted_iota(jnp.int32, (HD, T), 1)

    def query_features(d, j):
        q = (0, 1, 4, 5) if j == 0 else (2, 3, 6, 7)
        seg_row = ids(seg, chip(d), q)
        here = lax.shift_right_logical(half_pos, 8) * 8 + j * 4 + lax.shift_right_logical(half_pos & (SUB - 1), 6)
        hot = ((half_row < DOCS) & (seg_row == half_row)) | (
            (half_row >= DOCS) & (half_row < LSE_ROW) & (here == half_row - DOCS)
        )
        return jnp.where(hot, 1.0, 0.0)

    def with_lse(feat, stats):
        high, mid, low = thirds(stats)
        return jnp.where(
            half_row == LSE_ROW, high,
            jnp.where(half_row == LSE_ROW + 1, mid, jnp.where(half_row == LSE_ROW + 2, low, feat)),
        ).astype(BF16)

    def with_delta(stats):
        high, mid, low = thirds(stats)
        return jnp.where(
            half_row == 0, high, jnp.where(half_row == 1, mid, jnp.where(half_row == 2, low, 0.0))
        ).astype(BF16)

    for j in range(2):
        qt[j, :HD, :] = qw[0, j].reshape(T, HD).astype(F32).T.astype(BF16)
        qt[j, HD:, :] = query_features(0, j).astype(BF16)
    m_s[...] = jnp.full(m_s.shape, -1e30, F32)
    l_s[...] = jnp.zeros(l_s.shape, F32)
    ot[...] = jnp.zeros(ot.shape, F32)
    da[...] = jnp.zeros(da.shape, F32)

    def scores(qtr, d, h, start_row, count, features, own, first=0):
        rows = pl.ds(start_row, count)
        frows = pl.ds(h * T + start_row, count)
        k_tile = kv[d, h, 0, rows, :]
        s = dot(jnp.concatenate([k_tile, fk[features, frows, :]], axis=1), qtr)
        if own is not None:
            key_pos = h * T + start_row + lax.broadcasted_iota(jnp.int32, s.shape, 0)
            q = first + lax.broadcasted_iota(jnp.int32, s.shape, 1)
            query_pos = lax.shift_right_logical(q, 8) * T + own * SUB + (q & (SUB - 1))
            s = jnp.where(key_pos <= query_pos, s, -2.0 * MASK)
        return s, k_tile, kv[d, h, 1, rows, :]

    def spans(d, h):
        if (d, h) == (0, 1):
            return SUB, SUB
        if (d, h) == (REACH, 0):
            return 0, SUB
        return 0, T

    def forward(key):
        d, h = key
        q0, qn = spans(d, h)

        for j in range(2):
            qsl = slice(q0, q0 + qn)
            s, _, v_tile = scores(qt[j, :, qsl], d, h, 0, T, d, j if d == 0 else None, q0)
            old = m_s[j, :, qsl]
            new = jnp.maximum(old, jnp.max(s, axis=0, keepdims=True))
            p = jnp.exp2((s - new) * LOG2)
            fade = jnp.exp2((old - new) * LOG2)
            m_s[j, :, qsl] = new
            l_s[j, :, qsl] = l_s[j, :, qsl] * fade + jnp.sum(p, axis=0, keepdims=True)
            ot[j, :, qsl] = ot[j, :, qsl] * fade + dot_tn(v_tile, p.astype(BF16))

    order = (0, 1, -1, 2, -2, 3, -3, 4)

    def grad_blocks(j, indices):
        for index in indices:
            block = zed(order[index])
            w_cols = w_in[:, pl.ds(pl.multiple_of(block * T, T), T)]
            da[j] = da[j] + dot_nt(gmf[block, 2 * j:2 * j + 2].reshape(SUB, T), w_cols)

    mine = cols(c, HD)

    def grad_out(j):
        dos[j] = da[j, :, cols(o, HD)].astype(BF16)
        start(remote(dos.at[j], dow.at[0, j, c], do_s.at[j], do_r.at[j], sib, z))
        dow[0, j, c] = da[j, :, mine].astype(BF16)

    def grad_in(j):
        dst = dow.at[0, j, o]
        remote(dst, dst, do_s.at[j], do_r.at[j], sib, z).wait_recv()
        dts.first(j)

    def stats(j):
        rows = dow[0, j].reshape(T, HD).astype(F32).T
        dot_t[j, :HD, :] = rows.astype(BF16)
        st[0, j, 1:2, :] = jnp.sum(rows * otb[j].astype(F32), axis=0, keepdims=True)
        dot_t[j, HD:, :] = with_delta(st[0, j, 1:2, :])
        sts.first(j)

    def parts(qtr, dtr, d, h, features, own=None, first=0):
        s, k_tile, v_tile = scores(qtr, d, h, 0, T, features, own, first)
        p = jnp.exp2(s * LOG2)
        minus = jnp.where(lax.broadcasted_iota(jnp.int32, (T, HD), 1) < 3, -1.0, 0.0).astype(BF16)
        ds = p * dot(jnp.concatenate([v_tile, minus], axis=1), dtr)
        return k_tile, p.astype(BF16), ds.astype(BF16)

    def add_keys(h, p, ds, q_rows, do_rows):
        acc[h, 0] = acc[h, 0] + dot(ds, q_rows)
        acc[h, 1] = acc[h, 1] + dot(p, do_rows)

    def grad_query(j, d, h):
        q0, qn = spans(d, h)
        qsl = slice(q0, q0 + qn)
        own = j if d == 0 else None
        k_tile, p, ds = parts(qt[j, :, qsl], dot_t[j, :, qsl], d, h, d, own, q0)
        dqt[j, :, qsl] = dqt[j, :, qsl] + dot_tn(k_tile, ds)
        if d == 0:
            add_keys(h, p, ds, qw[0, j].reshape(T, HD)[q0:q0 + qn], dow[0, j].reshape(T, HD)[q0:q0 + qn])

    def grad_keys(j, d):
        qtmp[:HD, :] = qw[d, j].reshape(T, HD).astype(F32).T.astype(BF16)
        qtmp[HD:, :] = with_lse(query_features(d, j), st[d, j, 0:1, :])
        dtmp[:HD, :] = dow[d, j].reshape(T, HD).astype(F32).T.astype(BF16)
        dtmp[HD:, :] = with_delta(st[d, j, 1:2, :])
        for h in range(2):
            q0, qn = spans(d, h)
            _, p, ds = parts(qtmp[:, q0:q0 + qn], dtmp[:, q0:q0 + qn], 0, h, REACH + 1)
            add_keys(h, p, ds, qw[d, j].reshape(T, HD)[q0:q0 + qn], dow[d, j].reshape(T, HD)[q0:q0 + qn])

    def att_step(k):
        step, part = k // 2 + 1, k % 2
        ring_recv(atf, za_s, za_r, step, part, 2)
        ring_send(atf, za_s, za_r, step + 1, part, 2)

    per = nc // nz

    def weight_block(index):
        block = zed(order[index])
        pg[...] = dot_tn(atf[z, 0], gmf[block, 0:2].reshape(SUB, T)) + dot_tn(
            atf[z, 1], gmf[block, 2:4].reshape(SUB, T)
        )
        for e in range(per):
            gown[block * per + e] = pg[:, pl.ds(pl.multiple_of(e * SUB + c * HD, HD), HD)]
            gws[block * per + e] = pg[:, pl.ds(pl.multiple_of(e * SUB + o * HD, HD), HD)].astype(BF16)
        pair = pl.ds(block * per, per)
        start(remote(gws.at[pair], gwr.at[pair], gx_s.at[index], gx_r.at[index], sib, z))

    forward((0, 0))
    gm_step(0, 1)
    kvs.take(4, 0)
    forward((0, 1))
    gm_step(0, 2)
    kvs.take(4, 1)
    forward((4, 0))
    kvs.take(1, 0)
    kvs.take(3, 0)
    forward((4, 1))
    gm_step(0, 3)
    gm_send(1)
    kvs.take(1, 1)
    kvs.take(3, 1)
    forward((1, 0))
    grad_blocks(0, (0, 1, 2))
    gm_step(0, 4)
    grad_blocks(0, (3, 4, 5, 6, 7))
    grad_out(0)
    forward((3, 0))
    kvs.take(2, 0)
    for i in range(2):
        qts.first(i)

    @pl.loop(1, nz)
    def _(by):
        src = wsl.at[zed(-by), rows16, wide]
        remote(src, src, w1_s.at[by], w1_r.at[by], me, z).wait_recv()

    for by in range(1, NX):
        src = wsl.at[:, rows16, wide]
        start(remote(src, src, wx_s.at[by], wx_r.at[by], mate(0, by), z))
    gm_step(1, 1)
    grad_in(0)
    forward((1, 1))
    forward((3, 1))
    kvs.take(2, 1)
    qts.take(4, 0)
    qts.take(4, 1)
    gm_step(1, 2)
    forward((2, 0))
    forward((2, 1))

    for j in range(2):
        att = ot[j] * (1.0 / l_s[j])
        otb[j] = att.astype(BF16)
        st[0, j] = jnp.broadcast_to(m_s[j] + jnp.log2(l_s[j]) * (1.0 / LOG2), (8, T))
        for h in range(2):
            ob[h, j] = att[:, h * SUB:(h + 1) * SUB].T.astype(BF16)
    start(remote(ob.at[o], atf.at[z, :, :, mine], at_s, at_r, sib, z))
    stats(0)
    dts.take(4, 0)
    atf[z, :, :, mine] = ob[c]
    for j in range(2):
        qt[j, HD:, :] = with_lse(query_features(0, j), st[0, j, 0:1, :])
    for by in range(1, NX):
        src = wsl.at[:, pl.ds(pl.multiple_of((y * NX + lax.rem(x - by + NX, NX)) * 16, 16), 16), wide]
        remote(src, src, wx_s.at[by], wx_r.at[by], me, z).wait_recv()
    for by in range(1, ny):
        src = wsl.at[:, pl.ds(pl.multiple_of(y * NX * 16, 16), NX * 16), wide]
        start(remote(src, src, wy_s.at[by], wy_r.at[by], mate(by, 0), z))
    dqt[...] = jnp.zeros(dqt.shape, F32)
    acc[...] = jnp.zeros(acc.shape, F32)
    dst = atf.at[z, :, :, cols(o, HD)]
    remote(dst, dst, at_s, at_r, sib, z).wait_recv()
    gm_step(1, 3)
    for half in range(2):
        ring_send(atf, za_s, za_r, 1, half, 2)
    for i in range(2):
        qts.take(1, i)
        qts.take(3, i)
    dts.take(1, 0)
    dts.take(3, 0)
    sts.take(4, 0)
    grad_blocks(1, (0, 1, 2, 3, 4, 5, 6))
    for index in range(7):
        weight_block(index)
    grad_query(0, 0, 0)
    grad_query(0, 0, 1)
    for h in range(2):
        grad_query(0, 1, h)
        grad_query(0, 2, h)
    gm_step(1, 4)
    grad_blocks(1, (7,))
    grad_out(1)
    weight_block(7)
    sts.take(1, 0)
    sts.take(3, 0)
    att_step(0)
    grad_in(1)
    stats(1)
    for index in range(8):
        pair = pl.ds(zed(order[index]) * per, per)
        remote(gwr.at[pair], gwr.at[pair], gx_s.at[index], gx_r.at[index], sib, z).wait_recv()

    def row_of(by):
        return pl.ds(lax.rem(y + by, ny) * NX, NX)

    for by in range(1, ny):
        ysend[by] = (gown[row_of(by)] + gwr[row_of(by)].astype(F32)).astype(BF16)
        start(remote(ysend.at[by], yin.at[by], gy_s.at[by], gy_r.at[by], mate(by, 0), z))
    grad_keys(0, 4)
    att_step(1)
    for i in range(2):
        qts.take(2, i)
    dts.take(2, 0)
    sts.take(2, 0)
    for h in range(2):
        grad_query(0, 3, h)
    dts.take(4, 1)
    sts.take(4, 1)
    for h in range(2):
        grad_query(0, 4, h)
    att_step(2)
    grad_keys(0, 1)
    grad_keys(0, 3)
    for slot in (1, 3):
        dts.take(slot, 1)
        sts.take(slot, 1)
    att_step(3)

    for by in range(1, ny):
        src = wsl.at[:, pl.ds(pl.multiple_of(lax.rem(y - by + ny, ny) * NX * 16, 16), NX * 16), wide]
        remote(src, src, wy_s.at[by], wy_r.at[by], me, z).wait_recv()
    start(remote(wsl.at[:, :, wide], wsl.at[:, :, wide], w3_s, w3_r, sib, z))
    for h in range(2):
        grad_query(1, 0, h)
    for h in range(2):
        grad_query(1, 1, h)
    att_step(4)
    grad_keys(0, 2)
    for h in range(2):
        grad_query(1, 2, h)
    att_step(5)
    dts.take(2, 1)
    sts.take(2, 1)

    xown[...] = gown[row_of(0)] + gwr[row_of(0)].astype(F32)
    for by in range(1, ny):
        remote(yin.at[by], yin.at[by], gy_s.at[by], gy_r.at[by], me, z).wait_recv()
        xown[...] = xown[...] + yin[by].astype(F32)
    for by in range(1, NX):
        xsend[by] = xown[lax.rem(x + by, NX)].astype(BF16)
        start(remote(xsend.at[by], xin.at[by], gt_s.at[by], gt_r.at[by], mate(0, by), z))
    for d in (4, 1, 3, 2):
        grad_keys(1, d)

    outs = (dq_out, dk_out, dv_out)
    for h in range(2):
        fin[1, h] = (acc[h, 0] * SCALE).astype(BF16)
        fin[2, h] = acc[h, 1].astype(BF16)
    for t in (1, 2):
        start(remote(fin.at[t, o], outs[t].at[:, mine], fn_s.at[t], fn_r.at[t], sib, z))
        outs[t][:, mine] = fin[t, c]

    for d in (3, 4):
        for h in range(2):
            grad_query(1, d, h)
    for h in range(2):
        for j in range(2):
            fin[0, h, j * SUB:(j + 1) * SUB] = (dqt[j, :, h * SUB:(h + 1) * SUB] * SCALE).T.astype(BF16)
    start(remote(fin.at[0, o], dq_out.at[:, mine], fn_s.at[0], fn_r.at[0], sib, z))
    dq_out[:, mine] = fin[0, c]

    other = wsl.at[:, :, cols(o, SUB)]
    remote(other, other, w3_s, w3_r, sib, z).wait_recv()

    def out_block(block, first=False):
        for half in range(2):
            rows = slice(half * SUB, half * SUB + SUB)
            part = dot(atf[block, half], wsl[block])
            lo[rows, :] = part if first else lo[rows, :] + part

    out_block(z, True)
    for by in (1, -1, 2, -2, 3, -3):
        out_block(zed(by))

    total = xown[x]
    for by in range(1, NX):
        remote(xin.at[by], xin.at[by], gt_s.at[by], gt_r.at[by], me, z).wait_recv()
        total = total + xin[by].astype(F32)
    gw_out[...] = total

    att_step(6)
    att_step(7)
    out_block(zed(4))
    out[...] = lo[...].astype(BF16)
    for t in range(3):
        dst = outs[t].at[:, cols(o, HD)]
        remote(dst, dst, fn_s.at[t], fn_r.at[t], sib, z).wait_recv()

    for copy in sent:
        copy.wait_send()

    @pl.loop(1, nz)
    def _(by):
        src = wsl.at[z, rows16, wide]
        remote(src, src, w1_s.at[by], w1_r.at[by], me, zed(by)).wait_send()

    for tree in (kvs, qts, dts, sts):
        tree.drain()


def copy_kernel(*refs):
    for src, dst in zip(refs[:5], refs[5:]):
        dst[...] = src[...]


def body(nc, nz, queries, key_in, values, segment, tool_ids, out_weight, grad_mixed):
    width = out_weight.shape[1]
    vm = pltpu.VMEM
    dma = pltpu.SemaphoreType.DMA
    one = dma(())
    grads = (2, T, HD)
    halves = (2, 2, SUB, HD)
    scratch = [
        vm((REACH + 1, *halves), BF16),
        vm((REACH + 1, 2, 2, T, HD), BF16),
        vm((REACH + 2, CT, HD), BF16),
        vm((2, 2 * HD, T), BF16), vm((2 * HD, T), BF16),
        vm((2, 1, T), F32), vm((2, 1, T), F32),
        vm((2, HD, T), F32),
        vm((2, HD, T), BF16),
        vm(halves, BF16),
        vm((nz, 4, HD, T), BF16),
        vm((2, SUB, 2 * HD), F32),
        vm((2, SUB, HD), BF16),
        vm((REACH + 1, *halves), BF16),
        vm((2, 2 * HD, T), BF16), vm((2 * HD, T), BF16),
        vm((2, HD, T), F32),
        vm((nz, 2 * HD, T), BF16),
        vm((nz, 2, SUB, 2 * HD), BF16),
        vm((T, T), F32),
        vm((REACH + 1, 2, 8, T), F32),
        vm((2 * HD, width), BF16),
        vm((2, *grads), F32),
        vm((3, 2, T, HD), BF16),
        vm((2 * HD, T), F32),
        vm((nc, 2 * HD, HD), F32),
        vm((nc, 2 * HD, HD), BF16), vm((nc, 2 * HD, HD), BF16),
        vm((nc // NX, NX, 2 * HD, HD), BF16), vm((nc // NX, NX, 2 * HD, HD), BF16),
        vm((NX, 2 * HD, HD), F32),
        vm((NX, 2 * HD, HD), BF16), vm((NX, 2 * HD, HD), BF16),
        dma((3,)), dma((3,)),
        dma((7, 2)), dma((REACH + 1, 2)),
        dma((4 * nz,)), dma((4 * nz,)), dma((2 * nz,)), dma((2 * nz,)),
        dma((nz,)), dma((nz,)),
        dma((NX,)), dma((NX,)), dma((nc // NX,)), dma((nc // NX,)), one, one,
        one, one, dma((2,)), dma((2,)),
        dma((7, 2)), dma((REACH + 1, 2)),
        dma((7, 2)), dma((REACH + 1, 2)),
        dma((7, 2)), dma((REACH + 1, 2)),
        dma((3,)), dma((3,)), dma((nz,)), dma((nz,)),
        dma((nc // NX,)), dma((nc // NX,)), dma((NX,)), dma((NX,)), dma((5,)),
    ]
    results = pl.pallas_call(
        functools.partial(kernel, nc, nz),
        out_shape=(
            jax.ShapeDtypeStruct((T, width // nz), BF16),
            jax.ShapeDtypeStruct(queries.shape, BF16),
            jax.ShapeDtypeStruct(queries.shape, BF16),
            jax.ShapeDtypeStruct(queries.shape, BF16),
            jax.ShapeDtypeStruct((2 * HD, width // (2 * nc)), F32),
        ),
        in_specs=[pl.BlockSpec(memory_space=pltpu.VMEM)] * 2 + [pl.BlockSpec(memory_space=pl.ANY)] * 5,
        out_specs=[pl.BlockSpec(memory_space=pltpu.VMEM)] * 5,
        scratch_shapes=scratch,
        compiler_params=pltpu.CompilerParams(
            collective_id=0, has_side_effects=True, vmem_limit_bytes=58 * 1024 * 1024
        ),
        cost_estimate=pl.CostEstimate(
            flops=20_000_000_000, bytes_accessed=8_000_000, transcendentals=10_000_000
        ),
    )(
        segment.reshape(-1, HD), tool_ids.reshape(-1, HD),
        queries.reshape(2, SUB, 2 * HD), key_in, values, out_weight, grad_mixed.reshape(4, HD, width // nz),
    )
    return pl.pallas_call(
        copy_kernel,
        out_shape=tuple(jax.ShapeDtypeStruct(r.shape, r.dtype) for r in results),
        in_specs=[pl.BlockSpec(memory_space=pltpu.VMEM)] * 5,
        out_specs=[pl.BlockSpec(memory_space=pltpu.VMEM)] * 5,
    )(*results)


def solution(mesh):
    nc, nz = mesh.shape["ctx"] // 2, mesh.shape["head"]
    split = P("ctx", "head")
    return jax.shard_map(
        functools.partial(body, nc, nz),
        mesh=mesh,
        in_specs=(split, split, split, P(), P(), P("head", None), split),
        out_specs=(split, split, split, split, P("head", "ctx")),
        check_vma=False,
    )
```

time: 105 us -> 99.2 us (0.945)
  the two profiles are of different devices: /device:TPU:19 before, /device:TPU:31 now
where the time goes in v3:
time: 99.2 us; the launch traced here: 99 us
  Pallas kernels  98.4 us (99%)
    pallas_call x1, Pallas kernels, body(): pl.pallas_call(functools.partial(kernel, nc, nz), out_shape=(jax.ShapeDty...  96 us
    pallas_call x1, Pallas kernels, body(): pl.pallas_call(copy_kernel, out_shape=tuple((jax.ShapeDtypeStruct(r.shape...  2.41 us

profile of v3, /device:TPU:31, one launch (start us, length us, event | category | flops | bytes accessed | tf_op | source)
XLA Modules:
  0.0 99.0 jit_solution(534598339232616052)
XLA Ops:
  0.6 96.0 %shard_map.110 = (bf16[512,512]{1,0:T(8,128)(2,1)}, bf16[512,256]{1,0:T(8,128)(2,1)}, bf16[512,256]{1,0:T(8,128)(2,1)}, bf16[512,256]{1,0:T(8,128)(2,1)}, f32[256,128]{1,0:T(8,128)}) custom-call(s32[128,128]{1,0:T(8,128)} %bitcast.6, s32[128,128]{1,0:T(8,128)} %bitcast.7, bf16[2,256,256]{2,1,0:T(8,128)(2,1)} %bitcast.5, bf16[512,256]{1,0:T(8,128)(2,1)} %k_in.1, ...), custom_call_target="tpu_custom_call" | custom-call | flops 20000000000 | bytes 8000000 | tf_op jit(solution)/shard_map/pallas_call | solution.py:645
  96.6 2.4 %shard_map.111 = (bf16[512,512]{1,0:T(8,128)(2,1)}, bf16[512,256]{1,0:T(8,128)(2,1)}, bf16[512,256]{1,0:T(8,128)(2,1)}, bf16[512,256]{1,0:T(8,128)(2,1)}, f32[256,128]{1,0:T(8,128)}) custom-call(bf16[512,512]{1,0:T(8,128)(2,1)} %get-tuple-element.10.refs_0_, bf16[512,256]{1,0:T(8,128)(2,1)} %get-tuple-element.11.refs_1_, ...), custom_call_target="tpu_custom_call" | custom-call | tf_op jit(solution)/shard_map/pallas_call | solution.py:667

commit v4 on v3

--- a/solution.py
+++ b/solution.py
@@ -445,9 +445,25 @@
     for by in range(1, NX):
         src = wsl.at[:, pl.ds(pl.multiple_of((y * NX + lax.rem(x - by + NX, NX)) * 16, 16), 16), wide]
         remote(src, src, wx_s.at[by], wx_r.at[by], me, z).wait_recv()
-    for by in range(1, ny):
-        src = wsl.at[:, pl.ds(pl.multiple_of(y * NX * 16, 16), NX * 16), wide]
-        start(remote(src, src, wy_s.at[by], wy_r.at[by], mate(by, 0), z))
+    def w_rows(by):
+        return pl.ds(pl.multiple_of(lax.rem(y + by + ny, ny) * NX * 16, 16), NX * 16)
+
+    def w_copy(way, on):
+        if on:
+            src = wsl.at[pl.ds(way * (nz // 2), nz // 2), w_rows(2 * way - 1), wide]
+        else:
+            src = wsl.at[:, w_rows(0), wide]
+        return remote(src, src, wy_s.at[way, on], wy_r.at[way, on], mate(1 - 2 * way, 0), z)
+
+    def w_take(way, on):
+        if on:
+            dst = wsl.at[pl.ds(way * (nz // 2), nz // 2), w_rows(2), wide]
+        else:
+            dst = wsl.at[:, w_rows(2 * way - 1), wide]
+        remote(dst, dst, wy_s.at[way, on], wy_r.at[way, on], me, z).wait_recv()
+
+    for way in range(2):
+        start(w_copy(way, 0))
     dqt[...] = jnp.zeros(dqt.shape, F32)
     acc[...] = jnp.zeros(acc.shape, F32)
     dst = atf.at[z, :, :, cols(o, HD)]
@@ -482,18 +498,38 @@
         pair = pl.ds(zed(order[index]) * per, per)
         remote(gwr.at[pair], gwr.at[pair], gx_s.at[index], gx_r.at[index], sib, z).wait_recv()
 
-    def row_of(by):
-        return pl.ds(lax.rem(y + by, ny) * NX, NX)
-
-    for by in range(1, ny):
-        ysend[by] = (gown[row_of(by)] + gwr[row_of(by)].astype(F32)).astype(BF16)
-        start(remote(ysend.at[by], yin.at[by], gy_s.at[by], gy_r.at[by], mate(by, 0), z))
+    def pieces(by, half):
+        return pl.ds(lax.rem(y + by, ny) * NX + half * (NX // 2), NX // 2)
+
+    def share(by, half):
+        rows = pieces(by, half)
+        return gown[rows] + gwr[rows].astype(F32)
+
+    def y_copy(way, message):
+        to = mate(1 - 2 * way, 0)
+        return remote(
+            ysend.at[way, message], yin.at[way, message], gy_s.at[way, message], gy_r.at[way, message], to, z
+        )
+
+    def y_take(way, message):
+        y_copy(way, message).wait_recv()
+        return yin[way, message].astype(F32)
+
+    for way in range(2):
+        ysend[way, 0] = share(2, way).astype(BF16)
+        start(y_copy(way, 0))
+    for way in range(2):
+        ysend[way, 1] = share(1 + 2 * way, 1 - way).astype(BF16)
+        start(y_copy(way, 1))
     grad_keys(0, 4)
     att_step(1)
     for i in range(2):
         qts.take(2, i)
     dts.take(2, 0)
     sts.take(2, 0)
+    for way in range(2):
+        w_take(way, 0)
+        start(w_copy(way, 1))
     for h in range(2):
         grad_query(0, 3, h)
     dts.take(4, 1)
@@ -502,15 +538,17 @@
         grad_query(0, 4, h)
     att_step(2)
     grad_keys(0, 1)
+    for way in range(2):
+        ysend[way, 2] = (share(1 + 2 * way, way) + y_take(way, 0)).astype(BF16)
+        start(y_copy(way, 2))
     grad_keys(0, 3)
     for slot in (1, 3):
         dts.take(slot, 1)
         sts.take(slot, 1)
     att_step(3)
 
-    for by in range(1, ny):
-        src = wsl.at[:, pl.ds(pl.multiple_of(lax.rem(y - by + ny, ny) * NX * 16, 16), NX * 16), wide]
-        remote(src, src, wy_s.at[by], wy_r.at[by], me, z).wait_recv()
+    for way in range(2):
+        w_take(way, 1)
     start(remote(wsl.at[:, :, wide], wsl.at[:, :, wide], w3_s, w3_r, sib, z))
     for h in range(2):
         grad_query(1, 0, h)
@@ -524,10 +562,8 @@
     dts.take(2, 1)
     sts.take(2, 1)
 
-    xown[...] = gown[row_of(0)] + gwr[row_of(0)].astype(F32)
-    for by in range(1, ny):
-        remote(yin.at[by], yin.at[by], gy_s.at[by], gy_r.at[by], me, z).wait_recv()
-        xown[...] = xown[...] + yin[by].astype(F32)
+    for half in range(2):
+        xown[half * 2:half * 2 + 2] = share(0, half) + y_take(half, 2) + y_take(1 - half, 1)
     for by in range(1, NX):
         xsend[by] = xown[lax.rem(x + by, NX)].astype(BF16)
         start(remote(xsend.at[by], xin.at[by], gt_s.at[by], gt_r.at[by], mate(0, by), z))
@@ -627,20 +663,20 @@
         vm((2 * HD, T), F32),
         vm((nc, 2 * HD, HD), F32),
         vm((nc, 2 * HD, HD), BF16), vm((nc, 2 * HD, HD), BF16),
-        vm((nc // NX, NX, 2 * HD, HD), BF16), vm((nc // NX, NX, 2 * HD, HD), BF16),
+        vm((2, 3, NX // 2, 2 * HD, HD), BF16), vm((2, 3, NX // 2, 2 * HD, HD), BF16),
         vm((NX, 2 * HD, HD), F32),
         vm((NX, 2 * HD, HD), BF16), vm((NX, 2 * HD, HD), BF16),
         dma((3,)), dma((3,)),
         dma((7, 2)), dma((REACH + 1, 2)),
         dma((4 * nz,)), dma((4 * nz,)), dma((2 * nz,)), dma((2 * nz,)),
         dma((nz,)), dma((nz,)),
-        dma((NX,)), dma((NX,)), dma((nc // NX,)), dma((nc // NX,)), one, one,
+        dma((NX,)), dma((NX,)), dma((2, 2)), dma((2, 2)), one, one,
         one, one, dma((2,)), dma((2,)),
         dma((7, 2)), dma((REACH + 1, 2)),
         dma((7, 2)), dma((REACH + 1, 2)),
         dma((7, 2)), dma((REACH + 1, 2)),
         dma((3,)), dma((3,)), dma((nz,)), dma((nz,)),
-        dma((nc // NX,)), dma((nc // NX,)), dma((NX,)), dma((NX,)), dma((5,)),
+        dma((2, 3)), dma((2, 3)), dma((NX,)), dma((NX,)), dma((5,)),
     ]
     results = pl.pallas_call(
         functools.partial(kernel, nc, nz),

time: 99.2 us -> 97.9 us (0.987)
  the two profiles are of different devices: /device:TPU:31 before, /device:TPU:1 now
where the time goes in v4:
time: 97.9 us; the launch traced here: 97.7 us
  Pallas kernels  97 us (99%)
    pallas_call x1, Pallas kernels, body(): pl.pallas_call(functools.partial(kernel, nc, nz), out_shape=(jax.ShapeDty...  94.6 us
    pallas_call x1, Pallas kernels, body(): pl.pallas_call(copy_kernel, out_shape=tuple((jax.ShapeDtypeStruct(r.shape...  2.41 us

profile of v4, /device:TPU:1, one launch (start us, length us, event | category | flops | bytes accessed | tf_op | source)
XLA Modules:
  0.0 97.7 jit_solution(17698745278487612595)
XLA Ops:
  0.6 94.6 %shard_map.110 = (bf16[512,512]{1,0:T(8,128)(2,1)}, bf16[512,256]{1,0:T(8,128)(2,1)}, bf16[512,256]{1,0:T(8,128)(2,1)}, bf16[512,256]{1,0:T(8,128)(2,1)}, f32[256,128]{1,0:T(8,128)}) custom-call(s32[128,128]{1,0:T(8,128)} %bitcast.6, s32[128,128]{1,0:T(8,128)} %bitcast.7, bf16[2,256,256]{2,1,0:T(8,128)(2,1)} %bitcast.5, bf16[512,256]{1,0:T(8,128)(2,1)} %k_in.1, ...), custom_call_target="tpu_custom_call" | custom-call | flops 20000000000 | bytes 8000000 | tf_op jit(solution)/shard_map/pallas_call | solution.py:681
  95.3 2.4 %shard_map.111 = (bf16[512,512]{1,0:T(8,128)(2,1)}, bf16[512,256]{1,0:T(8,128)(2,1)}, bf16[512,256]{1,0:T(8,128)(2,1)}, bf16[512,256]{1,0:T(8,128)(2,1)}, f32[256,128]{1,0:T(8,128)}) custom-call(bf16[512,512]{1,0:T(8,128)(2,1)} %get-tuple-element.10.refs_0_, bf16[512,256]{1,0:T(8,128)(2,1)} %get-tuple-element.11.refs_1_, ...), custom_call_target="tpu_custom_call" | custom-call | tf_op jit(solution)/shard_map/pallas_call | solution.py:703
